TPU v7x, 256 devices: a whole 4x4x8 slice. The times are simulated.
256 devices in a mesh: row: 64 (over z, x, y_lo), col: 4 (over y_hi, core).
Axes of the slice: x: 4, y: 4 (y_hi: 2, y_lo: 2; y = y_hi * 2 + y_lo), z: 8, core: 2. Of those that a mesh axis runs over, the one named last changes fastest.
Arguments:
- features: float32 [98304, 256], P(('row', 'col')), may hold values from -6 to 6
- w_qkv: bfloat16 [256, 768], replicated, may hold values from -0.375 to 0.375
- w_out: bfloat16 [256, 256], replicated, may hold values from -0.375 to 0.375
- head_bias: float32 [4], replicated, may hold values from -3 to 1
- out_gain: float32 [256], replicated, may hold values from 0.1 to 1.9
- tile_rows: int32 [256, 256], P(('row', 'col')), may hold values from 0 to 767, as said below
- tile_cols: int32 [256, 256], P(('row', 'col')), may hold values from 0 to 767, as said below
- tile_masks: int32 [256, 256, 2048], P(('row', 'col')), may hold values from 0 to 255
- tile_count: int32 [256], P(('row', 'col')), may hold values from 1 to 256, as said below
Outputs:
- updated: float32 [98304, 256], P(('row', 'col'))
Inputs may be any that keep to these rules, and one draw needn't show every extreme that they name: `tile_rows`: list d = r * 4 + c names only destination tiles of blocks r * 4 to r * 4 + 4 - 1 and only source tiles of blocks whose index modulo 4 is c; within one list no tile appears twice. `tile_cols`: see tile_rows. `tile_count`: some list has all 256 slots live.
All inputs are finite; a program needn't handle non-finite values.
Results may differ from a plain program's by a relative error of at most 0.0042.
Values may be sent and summed in bfloat16 or wider, within the bound.
A program may use at most 192 MiB of HBM per device.

v0:
```python
import math

import jax
import jax.numpy as jnp
from jax import lax
from jax.sharding import PartitionSpec as P

TILE = 128


def local(
    features, w_qkv, w_out, head_bias, out_gain, tile_rows, tile_cols, tile_masks, tile_count
):
    node_count, feature_width = features.shape
    head_count = head_bias.shape[0]
    head_size = feature_width // head_count
    tile_size = TILE
    col_total = lax.axis_size("col")
    rounded = features.astype(jnp.bfloat16)
    projections = jnp.dot(rounded, w_qkv, preferred_element_type=jnp.float32).astype(jnp.bfloat16)
    queries = lax.all_gather(projections[:, :feature_width], "col", axis=0, tiled=True)
    keys, values = (
        lax.all_gather(
            projections[:, feature_width : 2 * feature_width], "row", axis=0, tiled=True
        ),
        lax.all_gather(projections[:, 2 * feature_width :], "row", axis=0, tiled=True),
    )
    row_tiles = queries.shape[0] // tile_size
    col_tiles = keys.shape[0] // tile_size
    block_tiles = node_count // tile_size
    q_tiles = queries.reshape(row_tiles, tile_size, head_count, head_size)
    k_tiles = keys.reshape(col_tiles, tile_size, head_count, head_size)
    v_tiles = values.reshape(col_tiles, tile_size, head_count, head_size)
    rows_local = tile_rows[0] % row_tiles
    source_block = tile_cols[0] // block_tiles
    cols_local = source_block // col_total * block_tiles + tile_cols[0] % block_tiles
    tile_total = tile_count[0]
    slot_total = tile_rows.shape[1]
    group_size = math.gcd(16, slot_total)
    score_scale = 1.0 / math.sqrt(head_size)
    bit_shift = jnp.arange(8, dtype=jnp.int32)
    row_ids = jnp.arange(row_tiles, dtype=jnp.int32)

    def group_step(turn_index, totals):
        numerator, denominator = totals
        first_slot = turn_index * group_size
        rows_group = lax.dynamic_slice_in_dim(rows_local, first_slot, group_size)
        cols_group = lax.dynamic_slice_in_dim(cols_local, first_slot, group_size)
        mask_words = lax.dynamic_slice_in_dim(tile_masks[0], first_slot, group_size, 0)
        words_shaped = mask_words.reshape(group_size, tile_size, tile_size // 8)
        mask_bits = jnp.bitwise_and(jnp.right_shift(words_shaped[..., None], bit_shift), 1)
        live_slot = first_slot + jnp.arange(group_size, dtype=jnp.int32) < tile_total
        edge_mask = mask_bits.reshape(group_size, tile_size, tile_size).astype(
            jnp.float32
        ) * live_slot[:, None, None].astype(jnp.float32)
        scores = jnp.einsum(
            "gihe,gjhe->ghij",
            q_tiles[rows_group],
            k_tiles[cols_group],
            preferred_element_type=jnp.float32,
        )
        weights = (
            jax.nn.sigmoid(scores * score_scale + head_bias[None, :, None, None])
            * edge_mask[:, None]
        )
        packed = weights.astype(jnp.bfloat16)
        partial_value = jnp.einsum(
            "ghij,gjhe->gihe", packed, v_tiles[cols_group], preferred_element_type=jnp.float32
        )
        row_select = (rows_group[:, None] == row_ids[None, :]).astype(jnp.float32)
        numerator = numerator + jnp.einsum(
            "gr,gihe->rihe", row_select, partial_value, precision=lax.Precision.HIGHEST
        )
        denominator = denominator + jnp.einsum(
            "gr,ghi->hri", row_select, jnp.sum(weights, axis=3), precision=lax.Precision.HIGHEST
        )
        return (numerator, denominator)

    turns = (tile_total + group_size - 1) // group_size
    start = (
        jnp.zeros((row_tiles, tile_size, head_count, head_size), jnp.float32),
        jnp.zeros((head_count, row_tiles, tile_size), jnp.float32),
    )
    numerator, denominator = lax.fori_loop(0, turns, group_step, start)
    numerator = numerator.reshape(row_tiles * tile_size, feature_width)
    denominator = denominator.reshape(head_count, row_tiles * tile_size)
    summed_numerator, summed_denominator = lax.psum((numerator, denominator), "col")
    col_index = lax.axis_index("col")
    own_numerator = lax.dynamic_slice_in_dim(
        summed_numerator, col_index * node_count, node_count, 0
    )
    own_denominator = lax.dynamic_slice_in_dim(
        summed_denominator, col_index * node_count, node_count, 1
    )
    divisor = jnp.transpose(1.0 + own_denominator)
    mixed = (
        (own_numerator.reshape(node_count, head_count, head_size) / divisor[:, :, None])
        .reshape(node_count, feature_width)
        .astype(jnp.bfloat16)
    )
    projected = jnp.dot(mixed, w_out, preferred_element_type=jnp.float32)
    inverse = lax.rsqrt(jnp.mean(projected * projected, axis=1, keepdims=True) + 1e-05)
    return features + out_gain * projected * inverse


def solution(mesh):
    placed = (
        P(("row", "col"), None),
        P(),
        P(),
        P(),
        P(),
        P(("row", "col"), None),
        P(("row", "col"), None),
        P(("row", "col"), None, None),
        P(("row", "col")),
    )
    return jax.shard_map(
        local, mesh=mesh, in_specs=placed, out_specs=P(("row", "col"), None), check_vma=False
    )
```

profile of v0, /device:TPU:1, one launch (start us, length us, event | category | flops | bytes accessed | tf_op | source)
XLA Modules:
  0.0 1428.1 jit_solution(16732224850455091191)
XLA Ops:
  6.5 1.0 copy-done
  7.5 1.3 convolution_convert_fusion
  8.8 0.8 fusion.34
  9.7 0.7 all-gather.5.cloned.1.call-update
  11.1 11.8 all_gather.10
  22.9 0.7 reshape.104
  23.7 273.5 %all-gather.3.cloned.1.call-done = bf16[24576,256]{1,0:T(8,128)(2,1)} async-done(((bf16[384,256]{1,0:T(8,128)(2,1)}), bf16[24576,256]{1,0:T(8,128)(2,1)}) %all-gather.3.cloned.1.call-update) | async-done | bytes 12582928 | tf_op jit(solution)/shard_map/all_gather | solution.py:26
  297.2 36.2 %reshape.103 = bf16[192,128,4,64]{3,2,1,0:T(4,128)(2,1)} reshape(bf16[24576,256]{1,0:T(8,128)(2,1)} %all-gather.3.cloned.1.call-done) | data formatting | bytes 25165824 | tf_op jit(solution)/shard_map/reshape | solution.py:33
  333.3 286.2 %all-gather.5.cloned.1.call-done = bf16[24576,256]{1,0:T(8,128)(2,1)} async-done(((bf16[384,256]{1,0:T(8,128)(2,1)}), bf16[24576,256]{1,0:T(8,128)(2,1)}) %all-gather.5.cloned.1.call-update) | async-done | bytes 12582928 | tf_op jit(solution)/shard_map/all_gather | solution.py:23
  619.5 36.1 %reshape.105 = bf16[192,128,4,64]{3,2,1,0:T(4,128)(2,1)} reshape(bf16[24576,256]{1,0:T(8,128)(2,1)} %all-gather.5.cloned.1.call-done) | data formatting | bytes 25165824 | tf_op jit(solution)/shard_map/reshape | solution.py:32
  655.7 1.5 broadcast_in_dim.8
  657.2 124.3 %while.13 = (s32[]{:T(128)}, f32[12,128,4,64]{1,0,3,2:T(8,128)}, f32[4,12,128]{2,1,0:T(8,128)S(1)}, s32[]{:T(128)}, s32[256]{0:T(256)S(1)}, /*index=5*/s32[256]{...) while((s32[]{:T(128)}, f32[12,128,4,64]{1,0,3,2:T(8,128)}, ...), condition=%wide.region_2.3_spmd.clone, body=%wide.region_0.2_spmd.clone.sunk | while | flops 354943488 | bytes 42986704 | solution.py:84
  657.2 1.1 constant_dynamic-slice_fusion.2
  658.3 0.4 shift_right_arithmetic.51
  658.9 0.7 compare_convert_fusion.2
  660.0 11.8 gather_fusion
  671.8 3.5 gather_fusion.1
  675.4 5.7 fusion.57
  681.1 10.5 gather_fusion.2
  691.6 2.5 fusion.58
  694.1 3.0 fusion.59
  697.1 1.3 copy-done.3
  698.6 1.1 constant_dynamic-slice_fusion.2
  699.7 0.4 shift_right_arithmetic.51
  700.1 0.3 copy.80
  700.4 0.7 compare_convert_fusion.2
  701.5 11.8 gather_fusion
  713.2 3.5 gather_fusion.1
  716.8 5.7 fusion.57
  722.5 10.5 gather_fusion.2
  733.0 2.5 fusion.58
  735.5 3.0 fusion.59
  738.6 1.3 copy-done.3
  740.1 1.1 constant_dynamic-slice_fusion.2
  741.1 0.4 shift_right_arithmetic.51
  741.8 0.7 compare_convert_fusion.2
  742.9 11.8 gather_fusion
  754.7 3.5 gather_fusion.1
  758.2 5.7 fusion.57
  763.9 10.5 gather_fusion.2
  774.5 2.5 fusion.58
  776.9 3.0 fusion.59
  780.0 1.3 copy-done.3
  781.5 3.5 copy.67
  785.2 553.2 %psum.15 = f32[4,1536]{1,0:T(4,128)S(1)} all-reduce(f32[4,1536]{1,0:T(4,128)S(1)} %bitcast.63), channel_id=1, replica_groups=mesh['row'=64,'col'=4] {'col'}, use_global_device_ids=true, to_apply=%region_4.5 | all-reduce | flops 6144 | bytes 49152 | tf_op jit(solution)/shard_map/psum | solution.py:87
  1338.4 80.8 %all-reduce.2.cloned.1.call-done = f32[1536,256]{0,1:T(8,128)} async-done(((f32[1536,256]{0,1:T(8,128)}), f32[1536,256]{0,1:T(8,128)}) %all-reduce.2.cloned.1.call-update) | async-done | bytes 1572880 | tf_op jit(solution)/shard_map/psum | solution.py:87
  1419.1 1.0 fusion.30
  1420.6 0.9 copy.39
  (75 shorter events, 3.1 us)
Async XLA Ops:
  6.5 1.0 copy-start
  6.5 290.6 %all-gather.3.cloned.1.call-start = ((), (), s32[]{:S(2)}) async-start(), calls=%async_computation | async-start | bytes 12779520 | tf_op jit(solution)/shard_map/all_gather | solution.py:26
  9.6 14.0 copy-start.8
  9.6 14.0 copy-start.9
  9.7 609.9 %all-gather.5.cloned.1.call-start = ((), (), s32[]{:S(2)}) async-start(), calls=%async_computation.1 | async-start | bytes 12779520 | tf_op jit(solution)/shard_map/all_gather | solution.py:23
  10.4 1408.7 %all-reduce.2.cloned.1.call-start = ((), (), s32[]{:S(2)}) async-start(), calls=%async_computation.2 | async-start | bytes 3145728 | tf_op jit(solution)/shard_map/psum | solution.py:87
  655.7 1.5 copy-start.11
  657.2 14.6 %copy-start.4 = (bf16[12,128,4,64]{3,2,1,0:T(4,128)(2,1)}, bf16[12,128,4,64]{3,2,1,0:T(4,128)(2,1)S(1)}, u32[]{:S(2)}) copy-start(bf16[12,128,4,64]{3,2,1,0:T(4,128)(2,1)S(1)} %get-tuple-element.296) | copy-start | bytes 2359300 | tf_op jit(solution)/shard_map/while
  691.6 2.5 copy-start.2
  694.1 4.5 copy-start.5
  697.1 1.3 copy-start.3
  698.6 14.6 %copy-start.4 = (bf16[12,128,4,64]{3,2,1,0:T(4,128)(2,1)}, bf16[12,128,4,64]{3,2,1,0:T(4,128)(2,1)S(1)}, u32[]{:S(2)}) copy-start(bf16[12,128,4,64]{3,2,1,0:T(4,128)(2,1)S(1)} %get-tuple-element.296) | copy-start | bytes 2359300 | tf_op jit(solution)/shard_map/while
  733.0 2.5 copy-start.2
  735.5 4.5 copy-start.5
  738.5 1.3 copy-start.3
  740.0 14.6 %copy-start.4 = (bf16[12,128,4,64]{3,2,1,0:T(4,128)(2,1)}, bf16[12,128,4,64]{3,2,1,0:T(4,128)(2,1)S(1)}, u32[]{:S(2)}) copy-start(bf16[12,128,4,64]{3,2,1,0:T(4,128)(2,1)S(1)} %get-tuple-element.296) | copy-start | bytes 2359300 | tf_op jit(solution)/shard_map/while
  774.5 2.5 copy-start.2
  776.9 4.5 copy-start.5
  780.0 1.3 copy-start.3
  781.5 3.5 copy-start.6
  784.9 635.2 %copy-start.7 = (bf16[256,256]{1,0:T(8,128)(2,1)S(1)}, bf16[256,256]{1,0:T(8,128)(2,1)}, u32[]{:S(2)}) copy-start(bf16[256,256]{1,0:T(8,128)(2,1)} %param.13) | copy-start | bytes 393220
  784.9 635.5 %copy-start.10 = (f32[256]{0:T(256)S(1)}, f32[256]{0:T(256)}, u32[]{:S(2)}) copy-start(f32[256]{0:T(256)} %param.15) | copy-start | bytes 3076
  785.0 636.6 %copy-start.1 = (bf16[256,768]{1,0:T(8,128)(2,1)S(1)}, bf16[256,768]{1,0:T(8,128)(2,1)}, u32[]{:S(2)}) copy-start(bf16[256,768]{1,0:T(8,128)(2,1)} %param.12) | copy-start | bytes 1179652
Sparse Core Ops, SparseCore 0:
  9.8 287.3 all-gather.2
  299.0 320.5 all-gather.4
  785.1 634.0 all-reduce.1
where the time goes:
time: 1430 us
  waiting for transfers between devices  641 us (45%)
  blocking collectives  565 us (40%)
  local copies, waits for them, and re-layouts  168 us (12%)
  matrix products  35.6 us (2%)
    psum x1, blocking collectives, local(): lax.psum((numerator, denominator), 'col')  553 us
    all_gather x1, waiting for transfers between devices, local(): lax.all_gather(projections[:, feature_width:2 * feature_width], 'row', ax...  286 us
    all_gather x1, waiting for transfers between devices, local(): lax.all_gather(projections[:, 2 * feature_width:], 'row', axis=0, tiled=T...  273 us
    psum x1, waiting for transfers between devices, local(): lax.psum((numerator, denominator), 'col')  80.8 us
    reshape x1, local copies, waits for them, and re-layouts, local(): v_tiles = values.reshape(col_tiles, tile_size, head_count, head_size)  36.2 us
    reshape x1, local copies, waits for them, and re-layouts, local(): k_tiles = keys.reshape(col_tiles, tile_size, head_count, head_size)  36.1 us
    gather x3, local copies, waits for them, and re-layouts, group_step(): k_tiles[cols_group]  35.3 us
    gather x3, local copies, waits for them, and re-layouts, group_step(): v_tiles[cols_group]  31.5 us
  transfers between devices with their start and end apart: 3, of which 3 were waited for; matrix products, arithmetic and copies ran while one was open for 3% of the time, Pallas kernels for 0%

commit v1 on v0

v1 whole, which is shorter than its diff:
```python
import functools

import jax
import jax.numpy as jnp
from jax import lax
from jax.experimental import pallas as pl
from jax.experimental.pallas import tpu as pltpu
from jax.sharding import PartitionSpec as P

TILE = 128
HEADS = 4
HEAD = 64
D = 256
STRIP = 16
TABLE = 384
NX, NY, NZ = 4, 4, 8
SITES = NX * NZ
NODES = 384
FIRST = 160
SECOND = NODES - FIRST
BLOCK = NODES // TILE
MESH = pl.DeviceIdType.MESH
NT = (((1,), (1,)), ((), ()))


def position():
    row, col = lax.axis_index("row"), lax.axis_index("col")
    return row // 8, row // 2 % 4, col // 2 * 2 + row % 2, col % 2


def device(z, x, y, core):
    return ((z * NX + x) * 2 + y % 2, y // 2 * 2 + core)


def meet(partners):
    barrier = pltpu.get_barrier_semaphore()
    for partner in partners:
        pl.semaphore_signal(barrier, inc=1, device_id=partner, device_id_type=MESH)
    pl.semaphore_wait(barrier, len(partners))


def site_partners(z, x, y, core):
    found = [device(z, x, y, 1 - core)]
    for d in range(1, NY):
        found += [device(z, x, (y + d) % NY, core), device(z, x, (y + d) % NY, 1 - core)]
    return found


def lane_order():
    node = lax.broadcasted_iota(jnp.int32, (TILE, TILE), 0)
    lane = lax.broadcasted_iota(jnp.int32, (TILE, TILE), 1)
    return node, lane % 16 * 8 + lane // 16


def exchange_kernel(
    features_ref, masks_ref, rows_ref, cols_ref, count_ref, weights_ref,
    gathered, values, stationary, words, table,
    queries, own, own_queries, wq, wv, bits, landed, sorted_slots, diagonal,
    query_send, query_recv, list_send, list_recv,
    ring_send, first_x, first_z, second_z, second_x, sibling_send, sibling_recv,
):
    z, x, y, core = position()
    y_lo, y_hi = y % 2, y // 2
    site = z * NX + x
    own[...] = features_ref[...].astype(jnp.bfloat16)
    meet(
        site_partners(z, x, y, core)
        + [device(z, (x + d) % NX, y, core) for d in (1, 2, 3)]
        + [device((z + d) % NZ, x, y, core) for d in (1, 7)]
    )

    my_list = y_hi * 2 + core
    home = y_lo == core
    partner = device(z, x, y_hi * 2 + core, y_lo)

    def to_partner(src, dst, k):
        return pltpu.make_async_remote_copy(
            src_ref=src, dst_ref=dst, send_sem=list_send.at[k], recv_sem=list_recv.at[k],
            device_id=partner, device_id_type=MESH,
        )

    def hand_over(src, dst, k):
        @pl.when(home)
        def _():
            pltpu.make_async_copy(src, dst, list_recv.at[k]).start()

        @pl.when(jnp.logical_not(home))
        def _():
            to_partner(src, dst, k).start()

    def handed(ref, k):
        pltpu.make_async_copy(ref, ref, list_recv.at[k]).wait()

    def rows(a_site, parity, low, count):
        return pl.ds(pl.multiple_of((a_site * 2 + parity) * NODES + low, 16), count)

    def remote(src, dst, send, recv, target):
        pltpu.make_async_remote_copy(
            src_ref=src, dst_ref=dst, send_sem=send, recv_sem=recv,
            device_id=target, device_id_type=MESH,
        ).start()

    def arrived(a_site, low, count, sem):
        here = gathered.at[rows(a_site, core, low, count)]
        pltpu.make_async_copy(here, here, sem).wait()

    def forward(a_site, low, count, send, recv, target):
        here = gathered.at[rows(a_site, core, low, count)]
        remote(here, here, send, recv, target)

    up, down = device((z + 1) % NZ, x, y, core), device((z + 7) % NZ, x, y, core)
    right, left = device(z, (x + 1) % NX, y, core), device(z, (x + 3) % NX, y, core)
    across = device(z, (x + 2) % NX, y, core)
    other = device(z, x, y, 1 - core)
    z_to, x_to = (up, down), (right, left)

    def share(a_site, low, count):
        forward(a_site, low, count, sibling_send.at[0], sibling_recv.at[0], other)

    def site_of(dz, dx):
        return (z + dz + NZ) % NZ * NX + (x + dx + NX) % NX

    hand_over(own, gathered.at[rows(site, y_lo, 0, NODES)], 0)
    handed(gathered.at[rows(site, core, 0, NODES)], 0)
    for s in range(2):
        forward(site, FIRST, SECOND, ring_send.at[s], second_z.at[s, 0], z_to[s])
        forward(site, 0, FIRST, ring_send.at[2 + s], first_x.at[s], x_to[s])
    forward(site, 0, FIRST, ring_send.at[4], first_x.at[2], across)
    for s in range(2):
        forward(site, FIRST, SECOND, ring_send.at[2 + s], second_x.at[0, s, 0], x_to[s])
        forward(site, 0, FIRST, ring_send.at[s], first_z.at[s, 0, 0], z_to[s])
    share(site, 0, NODES)

    wq[...] = jnp.transpose(weights_ref[:, 0:D])
    wv[...] = jnp.transpose(weights_ref[:, 2 * D : 3 * D])
    node, lane_node = lane_order()
    to_lanes = jnp.where(node == lane_node, 1.0, 0.0).astype(jnp.bfloat16)
    q = lax.dot_general(wq[...], own[...], NT, preferred_element_type=jnp.float32)
    q = q.astype(jnp.bfloat16) * jnp.bfloat16(0.0625)
    for t in range(BLOCK):
        own_queries[t] = jnp.dot(
            q[:, t * TILE : (t + 1) * TILE], to_lanes, preferred_element_type=jnp.float32
        ).astype(jnp.bfloat16)

    def to_queries(d):
        return pltpu.make_async_remote_copy(
            src_ref=own_queries, dst_ref=queries.at[my_list],
            send_sem=query_send.at[d], recv_sem=query_recv.at[my_list],
            device_id=device(z, x, (y_hi * 2 + core + d) % NY, y_lo), device_id_type=MESH,
        )

    @pl.when(home)
    def _():
        pltpu.make_async_copy(own_queries, queries.at[my_list], query_recv.at[my_list]).start()

    @pl.when(jnp.logical_not(home))
    def _():
        to_queries(0).start()

    for d in (1, 2, 3):
        to_queries(d).start()
    bits[...] = masks_ref[...].astype(jnp.float32).astype(jnp.bfloat16)
    hand_over(bits, landed, 1)
    diagonal[...] = jnp.zeros_like(diagonal)

    def fold(c):
        pltpu.make_async_copy(queries.at[c], queries.at[c], query_recv.at[c]).wait()
        for t in range(BLOCK):
            for h in range(HEADS):
                diagonal[h * HEAD : (h + 1) * HEAD, h * TILE : (h + 1) * TILE] = (
                    queries[c, t, h * HEAD : (h + 1) * HEAD, :]
                )
            stationary[c * BLOCK + t] = jnp.dot(
                weights_ref[:, D : 2 * D], diagonal[...], preferred_element_type=jnp.float32
            ).astype(jnp.bfloat16)

    def spread(c):
        words[c] = landed[:, c * TILE : (c + 1) * TILE].astype(jnp.float32).astype(jnp.int32)

    def swap_bit(b):
        step = 1 << b
        slots = words.shape[1]
        upper = (lax.broadcasted_iota(jnp.int32, (slots, TILE), 1) // step) % 2 == 1
        for c in range(words.shape[0]):
            if c & step == 0:
                low, high = words[c], words[c + step]
                words[c] = jnp.where(upper, pltpu.roll(high, step, 1), low)
                words[c + step] = jnp.where(upper, high, pltpu.roll(low, TILE - step, 1))

    def start_words():
        handed(landed, 1)
        for c in range(words.shape[0]):
            spread(c)

    def sort_slots():
        slots = rows_ref.shape[1]
        row_tiles = NY * BLOCK
        to, source = rows_ref[...].astype(jnp.float32), cols_ref[...].astype(jnp.float32)
        count = jnp.full((1, slots), count_ref[0], jnp.int32).astype(jnp.float32)
        slot = lax.broadcasted_iota(jnp.int32, (1, slots), 1).astype(jnp.float32)
        a = to - row_tiles * jnp.floor((to + 0.5) * (1.0 / row_tiles))
        b = BLOCK * jnp.floor((source + 0.5) * (1.0 / row_tiles)) + (
            source - BLOCK * jnp.floor((source + 0.5) * (1.0 / BLOCK))
        )
        a = jnp.where(slot < count, a, float(row_tiles))
        base = jnp.zeros_like(a)
        total = jnp.zeros((1, 1), jnp.float32)
        for tile in range(row_tiles):
            number = jnp.sum(jnp.where(a == tile, 1.0, 0.0), axis=1, keepdims=True)
            number = 2.0 * jnp.floor((number + 1.5) * 0.5)
            base += jnp.where(a > tile, number, 0.0)
            total += number
        across_lanes = jnp.broadcast_to(a, (slots, slots))
        down = jnp.transpose(across_lanes)
        earlier = lax.broadcasted_iota(jnp.int32, (slots, slots), 0) < lax.broadcasted_iota(
            jnp.int32, (slots, slots), 1
        )
        rank = jnp.sum(
            jnp.where((across_lanes == down) & earlier, 1.0, 0.0), axis=0, keepdims=True
        )
        at = jnp.where(a < row_tiles, base + rank, float(TABLE))
        at_down = jnp.transpose(jnp.broadcast_to(at, (TABLE, slots)))
        hit = at_down == lax.broadcasted_iota(jnp.int32, (slots, TABLE), 1).astype(jnp.float32)

        def pick(value):
            down = jnp.transpose(jnp.broadcast_to(value, (TABLE, slots)))
            return jnp.sum(jnp.where(hit, down, 0.0), axis=0, keepdims=True)

        sorted_slots[0:1, :] = (pick(slot + 1.0) - 1.0).astype(jnp.int32)
        sorted_slots[1:2, :] = pick(a).astype(jnp.int32)
        sorted_slots[2:3, :] = pick(b).astype(jnp.int32)
        sorted_slots[3:4, :] = jnp.broadcast_to(total * 0.5, (1, TABLE)).astype(jnp.int32)
        sorted_slots[4:8, :] = jnp.zeros((4, TABLE), jnp.int32)
        hand_over(sorted_slots, table, 2)

    X_OFF = (0, -1, 1, 2)
    Z_OFF = (0, -1, 1, -2, 2, -3, 3, 4)
    HALF1, HALF2 = FIRST // 2, SECOND // 2

    def second_z_step(t):
        for s in range(2):
            sign = -1 if s == 0 else 1
            if t < 4:
                a = site_of(sign * t, 0)
                arrived(a, FIRST, SECOND, second_z.at[s, t - 1])
                if t < 3:
                    forward(a, FIRST, SECOND, ring_send.at[s], second_z.at[s, t], z_to[s])
                else:
                    forward(a, FIRST + s * HALF2, HALF2, ring_send.at[s], second_z.at[s, 3], z_to[s])
                k = Z_OFF.index(sign * t)
                for e in range(2):
                    forward(a, FIRST, SECOND, ring_send.at[2 + e], second_x.at[k, e, 0], x_to[e])
                share(a, FIRST, SECOND)
        if t == 4:
            a = site_of(4, 0)
            for s in range(2):
                arrived(a, FIRST + s * HALF2, HALF2, second_z.at[s, 3])
            for e in range(2):
                forward(a, FIRST, SECOND, ring_send.at[2 + e], second_x.at[7, e, 0], x_to[e])
            share(a, FIRST, SECOND)

    def first_x_step():
        for k in range(3):
            a = site_of(0, X_OFF[k + 1])
            arrived(a, 0, FIRST, first_x.at[k])
            for s in range(2):
                forward(a, 0, FIRST, ring_send.at[s], first_z.at[s, 0, k + 1], z_to[s])
            share(a, 0, FIRST)

    def first_z_step(t, k):
        if t < 4:
            for s in range(2):
                sign = -1 if s == 0 else 1
                a = site_of(sign * t, X_OFF[k])
                arrived(a, 0, FIRST, first_z.at[s, t - 1, k])
                if t < 3:
                    forward(a, 0, FIRST, ring_send.at[s], first_z.at[s, t, k], z_to[s])
                else:
                    forward(a, s * HALF1, HALF1, ring_send.at[s], first_z.at[s, 3, k], z_to[s])
                share(a, 0, FIRST)
        else:
            a = site_of(4, X_OFF[k])
            for s in range(2):
                arrived(a, s * HALF1, HALF1, first_z.at[s, 3, k])
            share(a, 0, FIRST)

    def second_x_step(k):
        for e in range(2):
            sign = -1 if e == 0 else 1
            a = site_of(Z_OFF[k], sign)
            arrived(a, FIRST, SECOND, second_x.at[k, e, 0])
            forward(a, FIRST + e * HALF2, HALF2, ring_send.at[2 + e], second_x.at[k, e, 1], x_to[e])
            share(a, FIRST, SECOND)

    def second_x_end(k):
        a = site_of(Z_OFF[k], 2)
        for e in range(2):
            arrived(a, FIRST + e * HALF2, HALF2, second_x.at[k, e, 1])
        share(a, FIRST, SECOND)

    def project(depth, m):
        a = site_of(jnp.where(m < NX, depth, -depth), m % NX)
        start = pl.multiple_of((a * 2 + core) * NODES, NODES)
        tile = (a * 2 + core) * BLOCK
        v = lax.dot_general(
            wv[...], gathered[pl.ds(start, NODES), :], NT, preferred_element_type=jnp.float32
        ).astype(jnp.bfloat16)
        for t in range(BLOCK):
            values[tile + t] = v[:, t * TILE : (t + 1) * TILE]
        done = values.at[pl.ds(tile, BLOCK)]
        remote(done, done, sibling_send.at[1], sibling_recv.at[1], other)

    def drain(count, sem):
        pltpu.make_async_copy(gathered.at[pl.ds(0, count)], gathered.at[pl.ds(0, count)], sem).wait()

    def project_round(r):
        lax.fori_loop(0, NX if r in (0, 4) else 2 * NX, lambda m, _: (project(r, m), 0)[1], 0)

    sort_slots()
    second_z_step(1)
    first_x_step()
    second_z_step(2)
    second_x_step(0)
    fold(0)
    fold(1)
    second_z_step(3)
    fold(2)
    second_x_end(0)
    project_round(0)
    for r in range(1, 4):
        for k in range(NX):
            first_z_step(r, k)
        if r == 1:
            second_z_step(4)
        second_x_step(2 * r - 1)
        second_x_step(2 * r)
        second_x_end(2 * r - 1)
        second_x_end(2 * r)
        project_round(r)
        if r == 1:
            fold(3)
            start_words()
        elif r == 2:
            swap_bit(0)
            swap_bit(1)
        else:
            swap_bit(2)
            swap_bit(3)
    second_x_step(7)
    for k in range(NX):
        first_z_step(4, k)
    second_x_end(7)
    project_round(4)

    half_values = values.at[pl.ds(0, SITES * BLOCK)]
    pltpu.make_async_copy(half_values, half_values, sibling_recv.at[1]).wait()
    pltpu.make_async_copy(half_values, half_values, sibling_send.at[1]).wait()
    drain(SITES * NODES, sibling_recv.at[0])
    drain(SITES * NODES, sibling_send.at[0])
    z_rows = 3 * SECOND + HALF2 + NX * (3 * FIRST + HALF1)
    x_rows = FIRST + NZ * (SECOND + HALF2)
    for s in range(2):
        drain(z_rows, ring_send.at[s])
        drain(x_rows, ring_send.at[2 + s])
    drain(FIRST, ring_send.at[4])
    for d in range(1, NY):
        to_queries(d).wait_send()
    handed(table, 2)

    @pl.when(jnp.logical_not(home))
    def _():
        to_queries(0).wait_send()
        to_partner(own, gathered.at[rows(site, y_lo, 0, NODES)], 0).wait_send()
        to_partner(bits, landed, 1).wait_send()
        to_partner(sorted_slots, table, 2).wait_send()


def exchange(features, masks, tile_rows, tile_cols, tile_count, weights):
    slots, length = masks.shape
    vmem = pl.BlockSpec(memory_space=pltpu.VMEM)
    smem = pl.BlockSpec(memory_space=pltpu.SMEM)
    dma = pltpu.SemaphoreType.DMA
    half = jnp.bfloat16
    return pl.pallas_call(
        exchange_kernel,
        out_shape=(
            jax.ShapeDtypeStruct((SITES * 2 * NODES, D), half),
            jax.ShapeDtypeStruct((SITES * 2 * BLOCK, D, TILE), half),
            jax.ShapeDtypeStruct((NY * BLOCK, D, HEADS * TILE), half),
            jax.ShapeDtypeStruct((length // TILE, slots, TILE), jnp.int32),
            jax.ShapeDtypeStruct((8, TABLE), jnp.int32),
        ),
        in_specs=[vmem, vmem, vmem, vmem, smem, vmem],
        out_specs=(vmem,) * 5,
        scratch_shapes=[
            pltpu.VMEM((NY, BLOCK, D, TILE), half),
            pltpu.VMEM((NODES, D), half),
            pltpu.VMEM((BLOCK, D, TILE), half),
            pltpu.VMEM((D, D), half),
            pltpu.VMEM((D, D), half),
            pltpu.VMEM((slots, length), half),
            pltpu.VMEM((slots, length), half),
            pltpu.VMEM((8, TABLE), jnp.int32),
            pltpu.VMEM((D, HEADS * TILE), half),
            dma((NY,)), dma((NY,)), dma((3,)), dma((3,)),
            dma((5,)), dma((3,)), dma((2, 4, NX)), dma((2, 4)), dma((NZ, 2, 2)), dma((2,)), dma((2,)),
        ],
        compiler_params=pltpu.CompilerParams(
            collective_id=0, has_side_effects=True, vmem_limit_bytes=16 * 1024 * 1024
        ),
        name="exchange",
    )(features, masks, tile_rows, tile_cols, tile_count, weights)


def attention_kernel(
    table_ref, bias_ref, gathered, values, stationary, words,
    num_ref, den_ref, num_acc, den_acc, even_scores, odd_scores, even_weights, odd_weights,
):
    pairs = table_ref[3, 0]
    num_acc[...] = jnp.zeros_like(num_acc)
    den_acc[...] = jnp.zeros_like(den_acc)
    odd_weights[...] = jnp.zeros_like(odd_weights)
    bit_of = jnp.left_shift(jnp.int32(1), lax.broadcasted_iota(jnp.int32, (8, TILE), 0))
    half_bias = [bias_ref[h] * 0.5 for h in range(HEADS)]

    def score(p, scores):
        a = table_ref[1, 2 * p]
        sources = jnp.concatenate(
            [
                gathered[pl.ds(pl.multiple_of(table_ref[2, 2 * p + u] * TILE, TILE), TILE), :]
                for u in range(2)
            ],
            axis=0,
        )

        def part(half):
            lanes = slice(half * 2 * TILE, (half + 1) * 2 * TILE)
            scores[:, lanes] = jnp.dot(
                sources, stationary[a, :, lanes], preferred_element_type=jnp.float32
            )

        return [functools.partial(part, half) for half in range(2)]

    def weigh(p, scores, weights):
        a = table_ref[1, 2 * p]
        total = [jnp.zeros((8, TILE), jnp.float32) for _ in range(HEADS)]

        def part(u, groups):
            s = table_ref[0, 2 * p + u]
            live = jnp.where(s >= 0, bit_of, 0)
            s = jnp.maximum(s, 0)
            for g in groups:
                edge = [
                    (jnp.broadcast_to(words[w, pl.ds(s, 1), :], (8, TILE)) & live) != 0
                    for w in (2 * g, 2 * g + 1)
                ]
                here = slice(u * TILE + g * STRIP, u * TILE + (g + 1) * STRIP)
                for h in range(HEADS):
                    lanes = slice(h * TILE, (h + 1) * TILE)
                    twice = jnp.tanh(scores[here, lanes] + half_bias[h]) + 1.0
                    low = jnp.where(edge[0], twice[0:8], 0.0)
                    high = jnp.where(edge[1], twice[8:16], 0.0)
                    total[h] += low + high
                    weights[here, lanes] = jnp.concatenate([low, high], axis=0).astype(jnp.bfloat16)

        def finish():
            for h in range(HEADS):
                den_acc[a, h] += total[h]

        half = TILE // STRIP // 2
        return [
            functools.partial(part, u, range(v * half, (v + 1) * half))
            for u in range(2) for v in range(2)
        ] + [finish]

    def mix(p, weights):
        a = table_ref[1, 2 * p]
        source = [table_ref[2, 2 * p + u] for u in range(2)]

        def part(half):
            rows = slice(half * TILE, (half + 1) * TILE)
            v = jnp.concatenate([values[b, rows, :] for b in source], axis=1)
            both = jnp.dot(
                v, weights[:, half * 2 * TILE : (half + 1) * 2 * TILE],
                preferred_element_type=jnp.float32,
            )
            for side in range(2):
                start = half * TILE + side * HEAD
                num_acc[a, start : start + HEAD, :] += both[
                    side * HEAD : (side + 1) * HEAD, side * TILE : (side + 1) * TILE
                ]

        return [functools.partial(part, half) for half in range(2)]

    def together(scored, mixed, weighed):
        for k in range(2):
            scored[k]()
            weighed[2 * k]()
            mixed[k]()
            weighed[2 * k + 1]()
        weighed[4]()

    for part in score(0, even_scores):
        part()

    def turn(t, _):
        p = 2 * t
        together(
            score(p + 1, odd_scores), mix(jnp.maximum(p - 1, 0), odd_weights),
            weigh(p, even_scores, even_weights),
        )
        together(
            score(p + 2, even_scores), mix(p, even_weights),
            weigh(p + 1, odd_scores, odd_weights),
        )
        return 0

    turns = (pairs + 1) // 2
    lax.fori_loop(0, turns, turn, 0)
    for part in mix(jnp.maximum(2 * turns - 1, 0), odd_weights):
        part()
    num_ref[...] = (num_acc[...] * 0.5).astype(num_ref.dtype)
    den_ref[...] = jnp.sum(den_acc[...], axis=2) * 0.5


def attention(table, bias, gathered, values, stationary, words):
    row_tiles = stationary.shape[0]
    smem = pl.BlockSpec(memory_space=pltpu.SMEM)
    vmem = pl.BlockSpec(memory_space=pltpu.VMEM)
    return pl.pallas_call(
        attention_kernel,
        out_shape=(
            jax.ShapeDtypeStruct((row_tiles, D, TILE), jnp.bfloat16),
            jax.ShapeDtypeStruct((row_tiles, HEADS, TILE), jnp.float32),
        ),
        in_specs=[smem] * 2 + [vmem] * 4,
        out_specs=(vmem, vmem),
        scratch_shapes=[
            pltpu.VMEM((row_tiles, D, TILE), jnp.float32),
            pltpu.VMEM((row_tiles, HEADS, 8, TILE), jnp.float32),
            pltpu.VMEM((2 * TILE, HEADS * TILE), jnp.float32),
            pltpu.VMEM((2 * TILE, HEADS * TILE), jnp.float32),
            pltpu.VMEM((2 * TILE, HEADS * TILE), jnp.bfloat16),
            pltpu.VMEM((2 * TILE, HEADS * TILE), jnp.bfloat16),
        ],
        compiler_params=pltpu.CompilerParams(vmem_limit_bytes=16 * 1024 * 1024),
        name="attention",
    )(table, bias, gathered, values, stationary, words)


def finish_kernel(
    features_ref, num_ref, den_ref, w_ref, gain_ref, out_ref,
    nums, dens, send, recv,
):
    z, x, y, core = position()
    y_lo = y % 2
    meet(site_partners(z, x, y, core))
    home = y_lo == core

    def part(d, src, dst, k):
        c = (y + d) % NY
        return pltpu.make_async_remote_copy(
            src_ref=src.at[c], dst_ref=dst.at[y], send_sem=send.at[k, d], recv_sem=recv.at[k, y],
            device_id=device(z, x, c // 2 * 2 + core, c % 2), device_id_type=MESH,
        )

    pairs = ((num_ref, nums), (den_ref, dens))
    for d in (1, 2, 3):
        for k, (src, dst) in enumerate(pairs):
            part(d, src, dst, k).start()
    for k, (src, dst) in enumerate(pairs):
        @pl.when(home)
        def _():
            pltpu.make_async_copy(src.at[y], dst.at[y], recv.at[k, y]).start()

        @pl.when(jnp.logical_not(home))
        def _():
            part(0, src, dst, k).start()

    for c in range(NY):
        for k, (src, dst) in enumerate(pairs):
            pltpu.make_async_copy(dst.at[c], dst.at[c], recv.at[k, c]).wait()
    total = sum(nums[c].astype(jnp.float32) for c in range(NY))
    weight = 1.0 + sum(dens[c] for c in range(NY))
    gain = gain_ref[...]
    node, lane_node = lane_order()
    to_nodes = jnp.transpose(jnp.where(node == lane_node, 1.0, 0.0)).astype(jnp.bfloat16)
    for t in range(NODES // TILE):
        mixed = total[t].reshape(HEADS, HEAD, TILE) / weight[t].reshape(HEADS, 1, TILE)
        mixed = mixed.reshape(D, TILE).astype(jnp.bfloat16)
        mixed = jnp.dot(mixed, to_nodes, preferred_element_type=jnp.float32).astype(jnp.bfloat16)
        projected = lax.dot_general(
            mixed, w_ref[...], (((0,), (0,)), ((), ())), preferred_element_type=jnp.float32
        )
        square = jnp.mean(projected * projected, axis=1, keepdims=True)
        here = pl.ds(t * TILE, TILE)
        out_ref[here, :] = features_ref[here, :] + gain * projected * lax.rsqrt(square + 1e-05)
    for d in range(NY):
        for k, (src, dst) in enumerate(pairs):
            if d:
                part(d, src, dst, k).wait_send()
            else:
                @pl.when(jnp.logical_not(home))
                def _():
                    part(d, src, dst, k).wait_send()


def finish(features, numerator, denominator, w_out, gain):
    vmem = pl.BlockSpec(memory_space=pltpu.VMEM)
    hbm = pl.BlockSpec(memory_space=pl.ANY)
    dma = pltpu.SemaphoreType.DMA
    return pl.pallas_call(
        finish_kernel,
        out_shape=jax.ShapeDtypeStruct(features.shape, jnp.float32),
        in_specs=[vmem, hbm, hbm, vmem, vmem],
        out_specs=vmem,
        scratch_shapes=[
            pltpu.VMEM(numerator.shape, numerator.dtype),
            pltpu.VMEM(denominator.shape, denominator.dtype),
            dma((2, NY)), dma((2, NY)),
        ],
        compiler_params=pltpu.CompilerParams(
            collective_id=1, has_side_effects=True, vmem_limit_bytes=32 * 1024 * 1024
        ),
        name="finish",
    )(features, numerator, denominator, w_out, gain)


def local(
    features, w_qkv, w_out, head_bias, out_gain, tile_rows, tile_cols, tile_masks, tile_count
):
    block_tiles = features.shape[0] // TILE
    gathered, values, stationary, words, table = exchange(
        features, tile_masks[0], tile_rows, tile_cols, tile_count, w_qkv
    )
    numerator, denominator = attention(
        table, head_bias, gathered, values, stationary, words
    )
    return finish(
        features,
        numerator.reshape(NY, block_tiles, D, TILE),
        denominator.reshape(NY, block_tiles, HEADS, TILE),
        w_out, out_gain[None, :],
    )


def solution(mesh):
    placed = (
        P(("row", "col"), None),
        P(),
        P(),
        P(),
        P(),
        P(("row", "col"), None),
        P(("row", "col"), None),
        P(("row", "col"), None, None),
        P(("row", "col")),
    )
    return jax.shard_map(
        local, mesh=mesh, in_specs=placed, out_specs=P(("row", "col"), None), check_vma=False
    )
```

time: 1430 us -> 120 us (0.08)
  waiting for transfers between devices: 641 us -> 0 us
  blocking collectives: 565 us -> 0 us
  local copies, waits for them, and re-layouts: 168 us -> 6.34 us
  Pallas kernels: 0 us -> 111 us
  matrix products: 35.6 us -> 0 us
    all_gather x2 -> x0, waiting for transfers between devices: 560 us -> none  [the longest x1 286 us: local(): lax.all_gather(projections[:, feature_width:2 * feature_width], 'row', ax...]
    psum x1 -> x0, blocking collectives: 553 us -> none  [local(): lax.psum((numerator, denominator), 'col')]
    pallas_call x0 -> x3, Pallas kernels: none -> 111 us  [the longest x1 63.7 us: exchange(): pl.pallas_call(exchange_kernel, out_shape=(jax.ShapeDtypeStruct((SITES *...]
    psum x1 -> x0, waiting for transfers between devices: 80.8 us -> none  [local(): lax.psum((numerator, denominator), 'col')]
    gather x9 -> x0, local copies, waits for them, and re-layouts: 77.5 us -> none  [the longest x3 35.3 us: group_step(): k_tiles[cols_group]]
    reshape x3 -> x0, local copies, waits for them, and re-layouts: 73 us -> none  [the longest x1 36.2 us: local(): v_tiles = values.reshape(col_tiles, tile_size, head_count, head_size)]
    dot_general x14 -> x0, matrix products: 35.6 us -> none  [the longest x3 17.1 us: group_step(): jnp.einsum('gihe,gjhe->ghij', q_tiles[rows_group], k_tiles[cols_group], p...]
  transfers between devices with their start and end apart: 3 -> 0, of which waited for: 3 -> 0; matrix products, arithmetic and copies ran while one was open for 3% -> 0% of each run, Pallas kernels for 0% -> 0%
where the time goes in v1:
time: 120 us; the launch traced here: 118 us
  Pallas kernels  111 us (92%)
  local copies, waits for them, and re-layouts  6.34 us (5%)
    pallas_call x1, Pallas kernels, exchange(): pl.pallas_call(exchange_kernel, out_shape=(jax.ShapeDtypeStruct((SITES *...  63.7 us
    pallas_call x1, Pallas kernels, finish(): pl.pallas_call(finish_kernel, out_shape=jax.ShapeDtypeStruct(features.sha...  31.6 us
    pallas_call x1, Pallas kernels, attention(): pl.pallas_call(attention_kernel, out_shape=(jax.ShapeDtypeStruct((row_til...  15.9 us
    unnamed x19, local copies, waits for them, and re-layouts  6.34 us

profile of v1, /device:TPU:1, one launch (start us, length us, event | category | flops | bytes accessed | tf_op | source)
XLA Modules:
  0.0 118.3 jit_solution(11776431588522290564)
XLA Ops:
  0.7 0.0 copy-start
  0.7 1.6 %copy-done = s32[1,256,2048]{2,1,0:T(8,128)S(1)} copy-done((s32[1,256,2048]{2,1,0:T(8,128)S(1)}, s32[1,256,2048]{2,1,0:T(8,128)}, u32[]{:S(2)}) %copy-start) | copy-done | bytes 2097176
  2.2 0.0 copy-start.1
  2.2 1.0 copy-done.1
  3.2 0.0 copy-start.3
  3.2 1.0 copy-done.3
  4.2 0.0 copy-start.5
  4.2 0.7 copy-done.5
  4.9 0.0 copy-start.6
  4.9 0.7 copy-done.6
  5.6 63.7 %exchange.1 = (bf16[24576,256]{1,0:T(8,128)(2,1)S(1)}, bf16[192,256,128]{2,1,0:T(8,128)(2,1)S(1)}, bf16[12,256,512]{2,1,0:T(8,128)(2,1)S(1)}, s32[16,256,128]{2,1,0:T(8,128)S(1)}, s32[8,384]{1,0:T(8,128)S(1)}) custom-call(f32[384,256]{1,0:T(8,128)S(1)} %copy-done.1, s32[256,2048]{1,0:T(8,128)S(1)} %bitcast.4, s32[1,256]{1,0:T(1,128)S(1)} %copy-done.5, ...), custom_call_target="tpu_custom_call" | custom-call | tf_op jit(solution)/shard_map/exchange/pallas_call | solution.py:384
  69.3 0.0 copy-start.8
  69.3 0.6 copy-done.8
  70.0 0.0 copy-start.2
  70.0 0.0 copy-start.4
  70.0 0.0 copy-start.7
  70.0 15.9 %attention.1 = (bf16[12,256,128]{2,1,0:T(8,128)(2,1)S(1)}, f32[12,4,128]{2,1,0:T(4,128)S(1)}) custom-call(s32[8,384]{1,0:T(8,128)S(1)} %get-tuple-element.12.table_ref, f32[4]{0:T(128)S(1)} %copy-done.8, bf16[24576,256]{1,0:T(8,128)(2,1)S(1)} %get-tuple-element.13.gathered, bf16[192,256,128]{2,1,0:T(8,128)(2,1)S(1)} %get-tuple-element.14.values, ...), custom_call_target="tpu_custom_call" | custom-call | tf_op jit(solution)/shard_map/attention/pallas_call | solution.py:530
  85.9 0.0 copy-done.2
  85.9 0.0 copy-done.4
  85.9 0.0 copy-done.7
  85.9 31.6 %finish.1 = f32[384,256]{1,0:T(8,128)S(1)} custom-call(f32[384,256]{1,0:T(8,128)S(1)} %copy-done.2, bf16[4,3,256,128]{3,2,1,0:T(8,128)(2,1)S(1)} %bitcast.5, f32[4,3,4,128]{3,2,1,0:T(4,128)S(1)} %bitcast.6, bf16[256,256]{1,0:T(8,128)(2,1)S(1)} %copy-done.4, f32[1,256]{1,0:T(1,128)S(1)} %bitcast.7), custom_call_target="tpu_custom_call" | custom-call | tf_op jit(solution)/shard_map/finish/pallas_call | solution.py:612
  117.5 0.7 copy.12
Async XLA Ops:
  0.7 1.6 %copy-start = (s32[1,256,2048]{2,1,0:T(8,128)S(1)}, s32[1,256,2048]{2,1,0:T(8,128)}, u32[]{:S(2)}) copy-start(s32[1,256,2048]{2,1,0:T(8,128)} %param.16) | copy-start | bytes 6291460
  2.2 1.0 copy-start.1
  3.2 1.0 copy-start.3
  4.2 0.7 copy-start.5
  4.9 0.7 copy-start.6
  69.3 0.7 copy-start.8
  70.0 15.9 %copy-start.2 = (f32[384,256]{1,0:T(8,128)S(1)}, f32[384,256]{1,0:T(8,128)}, u32[]{:S(2)}) copy-start(f32[384,256]{1,0:T(8,128)} %features_ref.3) | copy-start | bytes 1179652
  70.0 15.9 %copy-start.4 = (bf16[256,256]{1,0:T(8,128)(2,1)S(1)}, bf16[256,256]{1,0:T(8,128)(2,1)}, u32[]{:S(2)}) copy-start(bf16[256,256]{1,0:T(8,128)(2,1)} %w_ref.1) | copy-start | bytes 393220
  70.0 15.9 %copy-start.7 = (f32[256]{0:T(256)S(1)}, f32[256]{0:T(256)}, u32[]{:S(2)}) copy-start(f32[256]{0:T(256)} %param.13) | copy-start | bytes 3076

commit v2 on v1

--- a/solution.py
+++ b/solution.py
@@ -32,10 +32,12 @@
     return ((z * NX + x) * 2 + y % 2, y // 2 * 2 + core)
 
 
-def meet(partners):
+def meet(partners, meanwhile=None):
     barrier = pltpu.get_barrier_semaphore()
     for partner in partners:
         pl.semaphore_signal(barrier, inc=1, device_id=partner, device_id_type=MESH)
+    if meanwhile is not None:
+        meanwhile()
     pl.semaphore_wait(barrier, len(partners))
 
 
@@ -62,11 +64,19 @@
     z, x, y, core = position()
     y_lo, y_hi = y % 2, y // 2
     site = z * NX + x
-    own[...] = features_ref[...].astype(jnp.bfloat16)
+
+    def setup():
+        own[...] = features_ref[...].astype(jnp.bfloat16)
+        wq[...] = jnp.transpose(weights_ref[:, 0:D])
+        wv[...] = jnp.transpose(weights_ref[:, 2 * D : 3 * D])
+        bits[...] = masks_ref[...].astype(jnp.float32).astype(jnp.bfloat16)
+        diagonal[...] = jnp.zeros_like(diagonal)
+
     meet(
         site_partners(z, x, y, core)
         + [device(z, (x + d) % NX, y, core) for d in (1, 2, 3)]
-        + [device((z + d) % NZ, x, y, core) for d in (1, 7)]
+        + [device((z + d) % NZ, x, y, core) for d in (1, 7)],
+        setup,
     )
 
     my_list = y_hi * 2 + core
@@ -114,33 +124,8 @@
     other = device(z, x, y, 1 - core)
     z_to, x_to = (up, down), (right, left)
 
-    def share(a_site, low, count):
-        forward(a_site, low, count, sibling_send.at[0], sibling_recv.at[0], other)
-
     def site_of(dz, dx):
         return (z + dz + NZ) % NZ * NX + (x + dx + NX) % NX
-
-    hand_over(own, gathered.at[rows(site, y_lo, 0, NODES)], 0)
-    handed(gathered.at[rows(site, core, 0, NODES)], 0)
-    for s in range(2):
-        forward(site, FIRST, SECOND, ring_send.at[s], second_z.at[s, 0], z_to[s])
-        forward(site, 0, FIRST, ring_send.at[2 + s], first_x.at[s], x_to[s])
-    forward(site, 0, FIRST, ring_send.at[4], first_x.at[2], across)
-    for s in range(2):
-        forward(site, FIRST, SECOND, ring_send.at[2 + s], second_x.at[0, s, 0], x_to[s])
-        forward(site, 0, FIRST, ring_send.at[s], first_z.at[s, 0, 0], z_to[s])
-    share(site, 0, NODES)
-
-    wq[...] = jnp.transpose(weights_ref[:, 0:D])
-    wv[...] = jnp.transpose(weights_ref[:, 2 * D : 3 * D])
-    node, lane_node = lane_order()
-    to_lanes = jnp.where(node == lane_node, 1.0, 0.0).astype(jnp.bfloat16)
-    q = lax.dot_general(wq[...], own[...], NT, preferred_element_type=jnp.float32)
-    q = q.astype(jnp.bfloat16) * jnp.bfloat16(0.0625)
-    for t in range(BLOCK):
-        own_queries[t] = jnp.dot(
-            q[:, t * TILE : (t + 1) * TILE], to_lanes, preferred_element_type=jnp.float32
-        ).astype(jnp.bfloat16)
 
     def to_queries(d):
         return pltpu.make_async_remote_copy(
@@ -149,30 +134,27 @@
             device_id=device(z, x, (y_hi * 2 + core + d) % NY, y_lo), device_id_type=MESH,
         )
 
-    @pl.when(home)
-    def _():
-        pltpu.make_async_copy(own_queries, queries.at[my_list], query_recv.at[my_list]).start()
-
-    @pl.when(jnp.logical_not(home))
-    def _():
-        to_queries(0).start()
-
-    for d in (1, 2, 3):
-        to_queries(d).start()
-    bits[...] = masks_ref[...].astype(jnp.float32).astype(jnp.bfloat16)
-    hand_over(bits, landed, 1)
-    diagonal[...] = jnp.zeros_like(diagonal)
-
-    def fold(c):
-        pltpu.make_async_copy(queries.at[c], queries.at[c], query_recv.at[c]).wait()
+    def prepare():
+        node, lane_node = lane_order()
+        to_lanes = jnp.where(node == lane_node, 1.0, 0.0).astype(jnp.bfloat16)
+        q = lax.dot_general(wq[...], own[...], NT, preferred_element_type=jnp.float32)
+        q = q.astype(jnp.bfloat16) * jnp.bfloat16(0.0625)
         for t in range(BLOCK):
-            for h in range(HEADS):
-                diagonal[h * HEAD : (h + 1) * HEAD, h * TILE : (h + 1) * TILE] = (
-                    queries[c, t, h * HEAD : (h + 1) * HEAD, :]
-                )
-            stationary[c * BLOCK + t] = jnp.dot(
-                weights_ref[:, D : 2 * D], diagonal[...], preferred_element_type=jnp.float32
+            own_queries[t] = jnp.dot(
+                q[:, t * TILE : (t + 1) * TILE], to_lanes, preferred_element_type=jnp.float32
             ).astype(jnp.bfloat16)
+        sort_slots()
+
+    def fold(c, t):
+        if t == 0:
+            pltpu.make_async_copy(queries.at[c], queries.at[c], query_recv.at[c]).wait()
+        for h in range(HEADS):
+            diagonal[h * HEAD : (h + 1) * HEAD, h * TILE : (h + 1) * TILE] = (
+                queries[c, t, h * HEAD : (h + 1) * HEAD, :]
+            )
+        stationary[c * BLOCK + t] = jnp.dot(
+            weights_ref[:, D : 2 * D], diagonal[...], preferred_element_type=jnp.float32
+        ).astype(jnp.bfloat16)
 
     def spread(c):
         words[c] = landed[:, c * TILE : (c + 1) * TILE].astype(jnp.float32).astype(jnp.int32)
@@ -231,7 +213,35 @@
         sorted_slots[2:3, :] = pick(b).astype(jnp.int32)
         sorted_slots[3:4, :] = jnp.broadcast_to(total * 0.5, (1, TABLE)).astype(jnp.int32)
         sorted_slots[4:8, :] = jnp.zeros((4, TABLE), jnp.int32)
-        hand_over(sorted_slots, table, 2)
+
+    hand_over(own, gathered.at[rows(site, y_lo, 0, NODES)], 0)
+
+    @pl.when(jnp.logical_not(home))
+    def _():
+        prepare()
+
+    handed(gathered.at[rows(site, core, 0, NODES)], 0)
+    for s in range(2):
+        forward(site, FIRST, SECOND, ring_send.at[s], second_z.at[s, 0], z_to[s])
+        forward(site, 0, FIRST, ring_send.at[2 + s], first_x.at[s], x_to[s])
+    forward(site, 0, FIRST, ring_send.at[4], first_x.at[2], across)
+    for s in range(2):
+        forward(site, FIRST, SECOND, ring_send.at[2 + s], second_x.at[0, s, 0], x_to[s])
+        forward(site, 0, FIRST, ring_send.at[s], first_z.at[s, 0, 0], z_to[s])
+
+    @pl.when(home)
+    def _():
+        prepare()
+        pltpu.make_async_copy(own_queries, queries.at[my_list], query_recv.at[my_list]).start()
+
+    @pl.when(jnp.logical_not(home))
+    def _():
+        to_queries(0).start()
+
+    for d in (1, 2, 3):
+        to_queries(d).start()
+    hand_over(bits, landed, 1)
+    hand_over(sorted_slots, table, 2)
 
     X_OFF = (0, -1, 1, 2)
     Z_OFF = (0, -1, 1, -2, 2, -3, 3, 4)
@@ -250,14 +260,12 @@
                 k = Z_OFF.index(sign * t)
                 for e in range(2):
                     forward(a, FIRST, SECOND, ring_send.at[2 + e], second_x.at[k, e, 0], x_to[e])
-                share(a, FIRST, SECOND)
         if t == 4:
             a = site_of(4, 0)
             for s in range(2):
                 arrived(a, FIRST + s * HALF2, HALF2, second_z.at[s, 3])
             for e in range(2):
                 forward(a, FIRST, SECOND, ring_send.at[2 + e], second_x.at[7, e, 0], x_to[e])
-            share(a, FIRST, SECOND)
 
     def first_x_step():
         for k in range(3):
@@ -265,7 +273,6 @@
             arrived(a, 0, FIRST, first_x.at[k])
             for s in range(2):
                 forward(a, 0, FIRST, ring_send.at[s], first_z.at[s, 0, k + 1], z_to[s])
-            share(a, 0, FIRST)
 
     def first_z_step(t, k):
         if t < 4:
@@ -277,12 +284,10 @@
                     forward(a, 0, FIRST, ring_send.at[s], first_z.at[s, t, k], z_to[s])
                 else:
                     forward(a, s * HALF1, HALF1, ring_send.at[s], first_z.at[s, 3, k], z_to[s])
-                share(a, 0, FIRST)
         else:
             a = site_of(4, X_OFF[k])
             for s in range(2):
                 arrived(a, s * HALF1, HALF1, first_z.at[s, 3, k])
-            share(a, 0, FIRST)
 
     def second_x_step(k):
         for e in range(2):
@@ -290,18 +295,50 @@
             a = site_of(Z_OFF[k], sign)
             arrived(a, FIRST, SECOND, second_x.at[k, e, 0])
             forward(a, FIRST + e * HALF2, HALF2, ring_send.at[2 + e], second_x.at[k, e, 1], x_to[e])
-            share(a, FIRST, SECOND)
 
     def second_x_end(k):
         a = site_of(Z_OFF[k], 2)
         for e in range(2):
             arrived(a, FIRST + e * HALF2, HALF2, second_x.at[k, e, 1])
-        share(a, FIRST, SECOND)
+
+    plan = [
+        [
+            [(second_z_step, 1)], [(first_x_step,)], [(second_z_step, 2)], [(second_x_step, 0)],
+            [(second_z_step, 3)], [(second_x_end, 0)],
+        ],
+        [
+            [(first_z_step, 1, 0), (second_x_step, 1)],
+            [(first_z_step, 1, 1), (second_z_step, 4), (second_x_step, 2)],
+            [(first_z_step, 1, 2), (second_x_end, 1)],
+            [(first_z_step, 1, 3), (second_x_end, 2)],
+        ],
+    ]
+    for t in (2, 3):
+        k = 2 * t - 1
+        plan.append([
+            [(first_z_step, t, 0)], [(second_x_step, k)], [(first_z_step, t, 1)],
+            [(second_x_step, k + 1)], [(first_z_step, t, 2)], [(second_x_end, k)],
+            [(first_z_step, t, 3)], [(second_x_end, k + 1)],
+        ])
+    plan.append([
+        [(first_z_step, 4, 0)], [(second_x_step, 7)], [(first_z_step, 4, 1)], [],
+        [(first_z_step, 4, 2)], [(second_x_end, 7)], [(first_z_step, 4, 3)], [],
+    ])
+
+    folds = [(fold, c, t) for c in range(NY) for t in range(BLOCK)]
+    for n, extra in enumerate(folds):
+        plan[2 + n // 8][n % 8].append(extra)
+    for at, extra in (
+        ((3, 4), (start_words,)), ((3, 6), (swap_bit, 0)), ((4, 0), (swap_bit, 1)),
+        ((4, 2), (swap_bit, 2)), ((4, 4), (swap_bit, 3)),
+    ):
+        plan[at[0]][at[1]].append(extra)
 
     def project(depth, m):
         a = site_of(jnp.where(m < NX, depth, -depth), m % NX)
         start = pl.multiple_of((a * 2 + core) * NODES, NODES)
         tile = (a * 2 + core) * BLOCK
+        forward(a, 0, NODES, sibling_send.at[0], sibling_recv.at[0], other)
         v = lax.dot_general(
             wv[...], gathered[pl.ds(start, NODES), :], NT, preferred_element_type=jnp.float32
         ).astype(jnp.bfloat16)
@@ -310,47 +347,27 @@
         done = values.at[pl.ds(tile, BLOCK)]
         remote(done, done, sibling_send.at[1], sibling_recv.at[1], other)
 
+    def turn(r, i):
+        for j, todo in enumerate(plan[r] if r < len(plan) else []):
+            if todo:
+                @pl.when(i == j)
+                def _():
+                    for step in todo:
+                        step[0](*step[1:])
+
+        if r:
+            project(r - 1, i)
+        return 0
+
     def drain(count, sem):
         pltpu.make_async_copy(gathered.at[pl.ds(0, count)], gathered.at[pl.ds(0, count)], sem).wait()
 
-    def project_round(r):
-        lax.fori_loop(0, NX if r in (0, 4) else 2 * NX, lambda m, _: (project(r, m), 0)[1], 0)
-
-    sort_slots()
-    second_z_step(1)
-    first_x_step()
-    second_z_step(2)
-    second_x_step(0)
-    fold(0)
-    fold(1)
-    second_z_step(3)
-    fold(2)
-    second_x_end(0)
-    project_round(0)
-    for r in range(1, 4):
-        for k in range(NX):
-            first_z_step(r, k)
-        if r == 1:
-            second_z_step(4)
-        second_x_step(2 * r - 1)
-        second_x_step(2 * r)
-        second_x_end(2 * r - 1)
-        second_x_end(2 * r)
-        project_round(r)
-        if r == 1:
-            fold(3)
-            start_words()
-        elif r == 2:
-            swap_bit(0)
-            swap_bit(1)
-        else:
-            swap_bit(2)
-            swap_bit(3)
-    second_x_step(7)
-    for k in range(NX):
-        first_z_step(4, k)
-    second_x_end(7)
-    project_round(4)
+    for todo in plan[0]:
+        for step in todo:
+            step[0](*step[1:])
+    for r in range(1, 6):
+        blocks = NX if r in (1, 5) else 2 * NX
+        lax.fori_loop(0, blocks, lambda i, _: turn(r, i), 0)
 
     half_values = values.at[pl.ds(0, SITES * BLOCK)]
     pltpu.make_async_copy(half_values, half_values, sibling_recv.at[1]).wait()
@@ -495,9 +512,9 @@
     def together(scored, mixed, weighed):
         for k in range(2):
             scored[k]()
-            weighed[2 * k]()
             mixed[k]()
-            weighed[2 * k + 1]()
+        for k in range(4):
+            weighed[k]()
         weighed[4]()
 
     for part in score(0, even_scores):

time: 120 us -> 115 us (0.958)
  the two profiles are of different devices: /device:TPU:1 before, /device:TPU:35 now
where the time goes in v2:
time: 115 us
  Pallas kernels  108 us (94%)
  local copies, waits for them, and re-layouts  6.34 us (6%)
    pallas_call x1, Pallas kernels, exchange(): pl.pallas_call(exchange_kernel, out_shape=(jax.ShapeDtypeStruct((SITES *...  58.7 us
    pallas_call x1, Pallas kernels, finish(): pl.pallas_call(finish_kernel, out_shape=jax.ShapeDtypeStruct(features.sha...  47.1 us
    unnamed x19, local copies, waits for them, and re-layouts  6.34 us
    pallas_call x1, Pallas kernels, attention(): pl.pallas_call(attention_kernel, out_shape=(jax.ShapeDtypeStruct((row_til...  2.41 us

profile of v2, /device:TPU:35, one launch (start us, length us, event | category | flops | bytes accessed | tf_op | source)
XLA Modules:
  0.0 115.2 jit_solution(4080108600474303615)
XLA Ops:
  0.7 0.0 copy-start
  0.7 1.6 %copy-done = s32[1,256,2048]{2,1,0:T(8,128)S(1)} copy-done((s32[1,256,2048]{2,1,0:T(8,128)S(1)}, s32[1,256,2048]{2,1,0:T(8,128)}, u32[]{:S(2)}) %copy-start) | copy-done | bytes 2097176
  2.2 0.0 copy-start.1
  2.2 1.0 copy-done.1
  3.2 0.0 copy-start.3
  3.2 1.0 copy-done.3
  4.2 0.0 copy-start.5
  4.2 0.7 copy-done.5
  4.9 0.0 copy-start.6
  4.9 0.7 copy-done.6
  5.6 58.7 %exchange.1 = (bf16[24576,256]{1,0:T(8,128)(2,1)S(1)}, bf16[192,256,128]{2,1,0:T(8,128)(2,1)S(1)}, bf16[12,256,512]{2,1,0:T(8,128)(2,1)S(1)}, s32[16,256,128]{2,1,0:T(8,128)S(1)}, s32[8,384]{1,0:T(8,128)S(1)}) custom-call(f32[384,256]{1,0:T(8,128)S(1)} %copy-done.1, s32[256,2048]{1,0:T(8,128)S(1)} %bitcast.4, s32[1,256]{1,0:T(1,128)S(1)} %copy-done.5, ...), custom_call_target="tpu_custom_call" | custom-call | tf_op jit(solution)/shard_map/exchange/pallas_call | solution.py:401
  64.3 0.0 copy-start.8
  64.3 0.6 copy-done.8
  64.9 0.0 copy-start.2
  64.9 0.0 copy-start.4
  64.9 0.0 copy-start.7
  64.9 2.4 %attention.1 = (bf16[12,256,128]{2,1,0:T(8,128)(2,1)S(1)}, f32[12,4,128]{2,1,0:T(4,128)S(1)}) custom-call(s32[8,384]{1,0:T(8,128)S(1)} %get-tuple-element.12.table_ref, f32[4]{0:T(128)S(1)} %copy-done.8, bf16[24576,256]{1,0:T(8,128)(2,1)S(1)} %get-tuple-element.13.gathered, bf16[192,256,128]{2,1,0:T(8,128)(2,1)S(1)} %get-tuple-element.14.values, ...), custom_call_target="tpu_custom_call" | custom-call | tf_op jit(solution)/shard_map/attention/pallas_call | solution.py:547
  67.4 0.0 copy-done.2
  67.4 0.0 copy-done.4
  67.4 0.0 copy-done.7
  67.4 47.1 %finish.1 = f32[384,256]{1,0:T(8,128)S(1)} custom-call(f32[384,256]{1,0:T(8,128)S(1)} %copy-done.2, bf16[4,3,256,128]{3,2,1,0:T(8,128)(2,1)S(1)} %bitcast.5, f32[4,3,4,128]{3,2,1,0:T(4,128)S(1)} %bitcast.6, bf16[256,256]{1,0:T(8,128)(2,1)S(1)} %copy-done.4, f32[1,256]{1,0:T(1,128)S(1)} %bitcast.7), custom_call_target="tpu_custom_call" | custom-call | tf_op jit(solution)/shard_map/finish/pallas_call | solution.py:629
  114.5 0.7 copy.12
Async XLA Ops:
  0.7 1.6 %copy-start = (s32[1,256,2048]{2,1,0:T(8,128)S(1)}, s32[1,256,2048]{2,1,0:T(8,128)}, u32[]{:S(2)}) copy-start(s32[1,256,2048]{2,1,0:T(8,128)} %param.16) | copy-start | bytes 6291460
  2.2 1.0 copy-start.1
  3.2 1.0 copy-start.3
  4.2 0.7 copy-start.5
  4.9 0.7 copy-start.6
  64.3 0.7 copy-start.8
  64.9 2.4 %copy-start.2 = (f32[384,256]{1,0:T(8,128)S(1)}, f32[384,256]{1,0:T(8,128)}, u32[]{:S(2)}) copy-start(f32[384,256]{1,0:T(8,128)} %features_ref.3) | copy-start | bytes 1179652
  64.9 2.4 %copy-start.4 = (bf16[256,256]{1,0:T(8,128)(2,1)S(1)}, bf16[256,256]{1,0:T(8,128)(2,1)}, u32[]{:S(2)}) copy-start(bf16[256,256]{1,0:T(8,128)(2,1)} %w_ref.1) | copy-start | bytes 393220
  64.9 2.4 %copy-start.7 = (f32[256]{0:T(256)S(1)}, f32[256]{0:T(256)}, u32[]{:S(2)}) copy-start(f32[256]{0:T(256)} %param.13) | copy-start | bytes 3076

commit v3 on v2

--- a/solution.py
+++ b/solution.py
@@ -267,8 +267,8 @@
             for e in range(2):
                 forward(a, FIRST, SECOND, ring_send.at[2 + e], second_x.at[7, e, 0], x_to[e])
 
-    def first_x_step():
-        for k in range(3):
+    def first_x_step(*which):
+        for k in which:
             a = site_of(0, X_OFF[k + 1])
             arrived(a, 0, FIRST, first_x.at[k])
             for s in range(2):
@@ -301,41 +301,8 @@
         for e in range(2):
             arrived(a, FIRST + e * HALF2, HALF2, second_x.at[k, e, 1])
 
-    plan = [
-        [
-            [(second_z_step, 1)], [(first_x_step,)], [(second_z_step, 2)], [(second_x_step, 0)],
-            [(second_z_step, 3)], [(second_x_end, 0)],
-        ],
-        [
-            [(first_z_step, 1, 0), (second_x_step, 1)],
-            [(first_z_step, 1, 1), (second_z_step, 4), (second_x_step, 2)],
-            [(first_z_step, 1, 2), (second_x_end, 1)],
-            [(first_z_step, 1, 3), (second_x_end, 2)],
-        ],
-    ]
-    for t in (2, 3):
-        k = 2 * t - 1
-        plan.append([
-            [(first_z_step, t, 0)], [(second_x_step, k)], [(first_z_step, t, 1)],
-            [(second_x_step, k + 1)], [(first_z_step, t, 2)], [(second_x_end, k)],
-            [(first_z_step, t, 3)], [(second_x_end, k + 1)],
-        ])
-    plan.append([
-        [(first_z_step, 4, 0)], [(second_x_step, 7)], [(first_z_step, 4, 1)], [],
-        [(first_z_step, 4, 2)], [(second_x_end, 7)], [(first_z_step, 4, 3)], [],
-    ])
-
-    folds = [(fold, c, t) for c in range(NY) for t in range(BLOCK)]
-    for n, extra in enumerate(folds):
-        plan[2 + n // 8][n % 8].append(extra)
-    for at, extra in (
-        ((3, 4), (start_words,)), ((3, 6), (swap_bit, 0)), ((4, 0), (swap_bit, 1)),
-        ((4, 2), (swap_bit, 2)), ((4, 4), (swap_bit, 3)),
-    ):
-        plan[at[0]][at[1]].append(extra)
-
-    def project(depth, m):
-        a = site_of(jnp.where(m < NX, depth, -depth), m % NX)
+    def project(dz, k):
+        a = site_of(dz, X_OFF[k])
         start = pl.multiple_of((a * 2 + core) * NODES, NODES)
         tile = (a * 2 + core) * BLOCK
         forward(a, 0, NODES, sibling_send.at[0], sibling_recv.at[0], other)
@@ -347,27 +314,30 @@
         done = values.at[pl.ds(tile, BLOCK)]
         remote(done, done, sibling_send.at[1], sibling_recv.at[1], other)
 
-    def turn(r, i):
-        for j, todo in enumerate(plan[r] if r < len(plan) else []):
-            if todo:
-                @pl.when(i == j)
-                def _():
-                    for step in todo:
-                        step[0](*step[1:])
-
-        if r:
-            project(r - 1, i)
-        return 0
-
     def drain(count, sem):
         pltpu.make_async_copy(gathered.at[pl.ds(0, count)], gathered.at[pl.ds(0, count)], sem).wait()
 
-    for todo in plan[0]:
-        for step in todo:
-            step[0](*step[1:])
-    for r in range(1, 6):
-        blocks = NX if r in (1, 5) else 2 * NX
-        lax.fori_loop(0, blocks, lambda i, _: turn(r, i), 0)
+    order = [
+        (project, 0, 0), (first_z_step, 1, 0), (second_z_step, 1), (project, -1, 0), (project, 1, 0),
+        (first_x_step, 0, 1), (first_x_step, 2), (second_x_step, 0), (project, 0, 1), (project, 0, 2),
+        (first_z_step, 2, 0), (fold, 0, 0), (fold, 0, 1), (fold, 0, 2), (fold, 1, 0), (fold, 1, 1),
+        (fold, 1, 2), (fold, 2, 0), (fold, 2, 1), (fold, 2, 2), (fold, 3, 0), (second_x_step, 1),
+        (second_x_step, 2), (fold, 3, 1), (fold, 3, 2), (second_x_end, 0), (project, 0, 3),
+        (second_z_step, 2), (project, -2, 0), (project, 2, 0), (first_z_step, 1, 1), (first_z_step, 1, 2),
+        (first_z_step, 1, 3), (project, -1, 1), (project, -1, 2), (project, 1, 1), (first_z_step, 3, 0),
+        (project, 1, 2), (start_words,), (second_x_end, 1), (project, -1, 3), (second_x_end, 2),
+        (project, 1, 3), (swap_bit, 0), (swap_bit, 1), (swap_bit, 2), (swap_bit, 3), (second_z_step, 3),
+        (project, -3, 0), (project, 3, 0), (second_x_step, 3), (second_x_step, 4), (first_z_step, 4, 0),
+        (first_z_step, 2, 1), (project, -2, 1), (first_z_step, 2, 2), (first_z_step, 2, 3), (project, -2, 2),
+        (project, 2, 1), (second_z_step, 4), (project, 2, 2), (project, 4, 0), (second_x_end, 3),
+        (project, -2, 3), (second_x_end, 4), (project, 2, 3), (second_x_step, 5), (first_z_step, 3, 1),
+        (second_x_step, 6), (project, -3, 1), (project, 3, 1), (first_z_step, 3, 2), (first_z_step, 3, 3),
+        (project, -3, 2), (project, 3, 2), (second_x_step, 7), (first_z_step, 4, 1), (project, 4, 1),
+        (second_x_end, 5), (project, -3, 3), (first_z_step, 4, 2), (project, 4, 2), (first_z_step, 4, 3),
+        (second_x_end, 6), (project, 3, 3), (second_x_end, 7), (project, 4, 3),
+    ]
+    for step in order:
+        step[0](*step[1:])
 
     half_values = values.at[pl.ds(0, SITES * BLOCK)]
     pltpu.make_async_copy(half_values, half_values, sibling_recv.at[1]).wait()
@@ -431,7 +401,7 @@
 
 def attention_kernel(
     table_ref, bias_ref, gathered, values, stationary, words,
-    num_ref, den_ref, num_acc, den_acc, even_scores, odd_scores, even_weights, odd_weights,
+    num_ref, den_ref, num_acc, den_acc, even_weights, odd_weights,
 ):
     pairs = table_ref[3, 0]
     num_acc[...] = jnp.zeros_like(num_acc)
@@ -440,8 +410,9 @@
     bit_of = jnp.left_shift(jnp.int32(1), lax.broadcasted_iota(jnp.int32, (8, TILE), 0))
     half_bias = [bias_ref[h] * 0.5 for h in range(HEADS)]
 
-    def score(p, scores):
+    def weigh(p, weights):
         a = table_ref[1, 2 * p]
+        slots = [table_ref[0, 2 * p + u] for u in range(2)]
         sources = jnp.concatenate(
             [
                 gathered[pl.ds(pl.multiple_of(table_ref[2, 2 * p + u] * TILE, TILE), TILE), :]
@@ -451,44 +422,34 @@
         )
 
         def part(half):
-            lanes = slice(half * 2 * TILE, (half + 1) * 2 * TILE)
-            scores[:, lanes] = jnp.dot(
-                sources, stationary[a, :, lanes], preferred_element_type=jnp.float32
+            scores = jnp.dot(
+                sources, stationary[a, :, half * 2 * TILE : (half + 1) * 2 * TILE],
+                preferred_element_type=jnp.float32,
             )
+            total = [jnp.zeros((8, TILE), jnp.float32) for _ in range(2)]
+            for u, s in enumerate(slots):
+                live = jnp.where(s >= 0, bit_of, 0)
+                s = jnp.maximum(s, 0)
+                for g in range(TILE // STRIP):
+                    edge = [
+                        (jnp.broadcast_to(words[w, pl.ds(s, 1), :], (8, TILE)) & live) != 0
+                        for w in (2 * g, 2 * g + 1)
+                    ]
+                    here = slice(u * TILE + g * STRIP, u * TILE + (g + 1) * STRIP)
+                    for side in range(2):
+                        h = half * 2 + side
+                        score = scores[here, side * TILE : (side + 1) * TILE]
+                        twice = jnp.tanh(score + half_bias[h]) + 1.0
+                        low = jnp.where(edge[0], twice[0:8], 0.0)
+                        high = jnp.where(edge[1], twice[8:16], 0.0)
+                        total[side] += low + high
+                        weights[here, h * TILE : (h + 1) * TILE] = jnp.concatenate(
+                            [low, high], axis=0
+                        ).astype(jnp.bfloat16)
+            for side in range(2):
+                den_acc[a, half * 2 + side] += total[side]
 
         return [functools.partial(part, half) for half in range(2)]
-
-    def weigh(p, scores, weights):
-        a = table_ref[1, 2 * p]
-        total = [jnp.zeros((8, TILE), jnp.float32) for _ in range(HEADS)]
-
-        def part(u, groups):
-            s = table_ref[0, 2 * p + u]
-            live = jnp.where(s >= 0, bit_of, 0)
-            s = jnp.maximum(s, 0)
-            for g in groups:
-                edge = [
-                    (jnp.broadcast_to(words[w, pl.ds(s, 1), :], (8, TILE)) & live) != 0
-                    for w in (2 * g, 2 * g + 1)
-                ]
-                here = slice(u * TILE + g * STRIP, u * TILE + (g + 1) * STRIP)
-                for h in range(HEADS):
-                    lanes = slice(h * TILE, (h + 1) * TILE)
-                    twice = jnp.tanh(scores[here, lanes] + half_bias[h]) + 1.0
-                    low = jnp.where(edge[0], twice[0:8], 0.0)
-                    high = jnp.where(edge[1], twice[8:16], 0.0)
-                    total[h] += low + high
-                    weights[here, lanes] = jnp.concatenate([low, high], axis=0).astype(jnp.bfloat16)
-
-        def finish():
-            for h in range(HEADS):
-                den_acc[a, h] += total[h]
-
-        half = TILE // STRIP // 2
-        return [
-            functools.partial(part, u, range(v * half, (v + 1) * half))
-            for u in range(2) for v in range(2)
-        ] + [finish]
 
     def mix(p, weights):
         a = table_ref[1, 2 * p]
@@ -509,27 +470,15 @@
 
         return [functools.partial(part, half) for half in range(2)]
 
-    def together(scored, mixed, weighed):
+    def together(weighed, mixed):
         for k in range(2):
-            scored[k]()
+            weighed[k]()
             mixed[k]()
-        for k in range(4):
-            weighed[k]()
-        weighed[4]()
-
-    for part in score(0, even_scores):
-        part()
 
     def turn(t, _):
         p = 2 * t
-        together(
-            score(p + 1, odd_scores), mix(jnp.maximum(p - 1, 0), odd_weights),
-            weigh(p, even_scores, even_weights),
-        )
-        together(
-            score(p + 2, even_scores), mix(p, even_weights),
-            weigh(p + 1, odd_scores, odd_weights),
-        )
+        together(weigh(p, even_weights), mix(jnp.maximum(p - 1, 0), odd_weights))
+        together(weigh(p + 1, odd_weights), mix(p, even_weights))
         return 0
 
     turns = (pairs + 1) // 2
@@ -555,8 +504,6 @@
         scratch_shapes=[
             pltpu.VMEM((row_tiles, D, TILE), jnp.float32),
             pltpu.VMEM((row_tiles, HEADS, 8, TILE), jnp.float32),
-            pltpu.VMEM((2 * TILE, HEADS * TILE), jnp.float32),
-            pltpu.VMEM((2 * TILE, HEADS * TILE), jnp.float32),
             pltpu.VMEM((2 * TILE, HEADS * TILE), jnp.bfloat16),
             pltpu.VMEM((2 * TILE, HEADS * TILE), jnp.bfloat16),
         ],

time: 115 us -> 112 us (0.974)
  the two profiles are of different devices: /device:TPU:35 before, /device:TPU:1 now
where the time goes in v3:
time: 112 us
  Pallas kernels  105 us (94%)
  local copies, waits for them, and re-layouts  6.34 us (6%)
    pallas_call x1, Pallas kernels, exchange(): pl.pallas_call(exchange_kernel, out_shape=(jax.ShapeDtypeStruct((SITES *...  54.1 us
    pallas_call x1, Pallas kernels, attention(): pl.pallas_call(attention_kernel, out_shape=(jax.ShapeDtypeStruct((row_til...  36.8 us
    pallas_call x1, Pallas kernels, finish(): pl.pallas_call(finish_kernel, out_shape=jax.ShapeDtypeStruct(features.sha...  13.9 us
    unnamed x19, local copies, waits for them, and re-layouts  6.34 us

profile of v3, /device:TPU:1, one launch (start us, length us, event | category | flops | bytes accessed | tf_op | source)
XLA Modules:
  0.0 111.9 jit_solution(4259907725587505938)
XLA Ops:
  0.7 0.0 copy-start
  0.7 1.6 %copy-done = s32[1,256,2048]{2,1,0:T(8,128)S(1)} copy-done((s32[1,256,2048]{2,1,0:T(8,128)S(1)}, s32[1,256,2048]{2,1,0:T(8,128)}, u32[]{:S(2)}) %copy-start) | copy-done | bytes 2097176
  2.2 0.0 copy-start.1
  2.2 1.0 copy-done.1
  3.2 0.0 copy-start.3
  3.2 1.0 copy-done.3
  4.2 0.0 copy-start.5
  4.2 0.7 copy-done.5
  4.9 0.0 copy-start.6
  4.9 0.7 copy-done.6
  5.6 54.1 %exchange.1 = (bf16[24576,256]{1,0:T(8,128)(2,1)S(1)}, bf16[192,256,128]{2,1,0:T(8,128)(2,1)S(1)}, bf16[12,256,512]{2,1,0:T(8,128)(2,1)S(1)}, s32[16,256,128]{2,1,0:T(8,128)S(1)}, s32[8,384]{1,0:T(8,128)S(1)}) custom-call(f32[384,256]{1,0:T(8,128)S(1)} %copy-done.1, s32[256,2048]{1,0:T(8,128)S(1)} %bitcast.4, s32[1,256]{1,0:T(1,128)S(1)} %copy-done.5, ...), custom_call_target="tpu_custom_call" | custom-call | tf_op jit(solution)/shard_map/exchange/pallas_call | solution.py:371
  59.7 0.0 copy-start.8
  59.7 0.6 copy-done.8
  60.3 0.0 copy-start.2
  60.3 0.0 copy-start.4
  60.3 0.0 copy-start.7
  60.3 36.8 %attention.1 = (bf16[12,256,128]{2,1,0:T(8,128)(2,1)S(1)}, f32[12,4,128]{2,1,0:T(4,128)S(1)}) custom-call(s32[8,384]{1,0:T(8,128)S(1)} %get-tuple-element.12.table_ref, f32[4]{0:T(128)S(1)} %copy-done.8, bf16[24576,256]{1,0:T(8,128)(2,1)S(1)} %get-tuple-element.13.gathered, bf16[192,256,128]{2,1,0:T(8,128)(2,1)S(1)} %get-tuple-element.14.values, ...), custom_call_target="tpu_custom_call" | custom-call | tf_op jit(solution)/shard_map/attention/pallas_call | solution.py:496
  97.2 0.0 copy-done.2
  97.2 0.0 copy-done.4
  97.2 0.0 copy-done.7
  97.2 13.9 %finish.1 = f32[384,256]{1,0:T(8,128)S(1)} custom-call(f32[384,256]{1,0:T(8,128)S(1)} %copy-done.2, bf16[4,3,256,128]{3,2,1,0:T(8,128)(2,1)S(1)} %bitcast.5, f32[4,3,4,128]{3,2,1,0:T(4,128)S(1)} %bitcast.6, bf16[256,256]{1,0:T(8,128)(2,1)S(1)} %copy-done.4, f32[1,256]{1,0:T(1,128)S(1)} %bitcast.7), custom_call_target="tpu_custom_call" | custom-call | tf_op jit(solution)/shard_map/finish/pallas_call | solution.py:576
  111.1 0.7 copy.12
Async XLA Ops:
  0.7 1.6 %copy-start = (s32[1,256,2048]{2,1,0:T(8,128)S(1)}, s32[1,256,2048]{2,1,0:T(8,128)}, u32[]{:S(2)}) copy-start(s32[1,256,2048]{2,1,0:T(8,128)} %param.16) | copy-start | bytes 6291460
  2.2 1.0 copy-start.1
  3.2 1.0 copy-start.3
  4.2 0.7 copy-start.5
  4.9 0.7 copy-start.6
  59.7 0.7 copy-start.8
  60.3 36.8 %copy-start.2 = (f32[384,256]{1,0:T(8,128)S(1)}, f32[384,256]{1,0:T(8,128)}, u32[]{:S(2)}) copy-start(f32[384,256]{1,0:T(8,128)} %features_ref.3) | copy-start | bytes 1179652
  60.3 36.8 %copy-start.4 = (bf16[256,256]{1,0:T(8,128)(2,1)S(1)}, bf16[256,256]{1,0:T(8,128)(2,1)}, u32[]{:S(2)}) copy-start(bf16[256,256]{1,0:T(8,128)(2,1)} %w_ref.1) | copy-start | bytes 393220
  60.3 36.8 %copy-start.7 = (f32[256]{0:T(256)S(1)}, f32[256]{0:T(256)}, u32[]{:S(2)}) copy-start(f32[256]{0:T(256)} %param.13) | copy-start | bytes 3076

commit v4 on v3

--- a/solution.py
+++ b/solution.py
@@ -12,6 +12,7 @@
 HEAD = 64
 D = 256
 STRIP = 16
+UNROLL = 4
 TABLE = 384
 NX, NY, NZ = 4, 4, 8
 SITES = NX * NZ
@@ -318,23 +319,23 @@
         pltpu.make_async_copy(gathered.at[pl.ds(0, count)], gathered.at[pl.ds(0, count)], sem).wait()
 
     order = [
-        (project, 0, 0), (first_z_step, 1, 0), (second_z_step, 1), (project, -1, 0), (project, 1, 0),
-        (first_x_step, 0, 1), (first_x_step, 2), (second_x_step, 0), (project, 0, 1), (project, 0, 2),
-        (first_z_step, 2, 0), (fold, 0, 0), (fold, 0, 1), (fold, 0, 2), (fold, 1, 0), (fold, 1, 1),
-        (fold, 1, 2), (fold, 2, 0), (fold, 2, 1), (fold, 2, 2), (fold, 3, 0), (second_x_step, 1),
-        (second_x_step, 2), (fold, 3, 1), (fold, 3, 2), (second_x_end, 0), (project, 0, 3),
-        (second_z_step, 2), (project, -2, 0), (project, 2, 0), (first_z_step, 1, 1), (first_z_step, 1, 2),
-        (first_z_step, 1, 3), (project, -1, 1), (project, -1, 2), (project, 1, 1), (first_z_step, 3, 0),
-        (project, 1, 2), (start_words,), (second_x_end, 1), (project, -1, 3), (second_x_end, 2),
-        (project, 1, 3), (swap_bit, 0), (swap_bit, 1), (swap_bit, 2), (swap_bit, 3), (second_z_step, 3),
-        (project, -3, 0), (project, 3, 0), (second_x_step, 3), (second_x_step, 4), (first_z_step, 4, 0),
-        (first_z_step, 2, 1), (project, -2, 1), (first_z_step, 2, 2), (first_z_step, 2, 3), (project, -2, 2),
-        (project, 2, 1), (second_z_step, 4), (project, 2, 2), (project, 4, 0), (second_x_end, 3),
-        (project, -2, 3), (second_x_end, 4), (project, 2, 3), (second_x_step, 5), (first_z_step, 3, 1),
-        (second_x_step, 6), (project, -3, 1), (project, 3, 1), (first_z_step, 3, 2), (first_z_step, 3, 3),
-        (project, -3, 2), (project, 3, 2), (second_x_step, 7), (first_z_step, 4, 1), (project, 4, 1),
-        (second_x_end, 5), (project, -3, 3), (first_z_step, 4, 2), (project, 4, 2), (first_z_step, 4, 3),
-        (second_x_end, 6), (project, 3, 3), (second_x_end, 7), (project, 4, 3),
+        (second_z_step, 1), (fold, 0, 0), (fold, 0, 1), (fold, 0, 2), (first_z_step, 1, 0), (first_x_step, 2),
+        (second_x_step, 0), (first_x_step, 0, 1), (second_z_step, 2), (start_words,), (fold, 1, 0),
+        (swap_bit, 0), (project, 0, 0), (project, 0, 1), (first_z_step, 2, 0), (first_z_step, 1, 1),
+        (first_z_step, 1, 2), (second_x_step, 1), (project, -1, 1), (fold, 1, 1), (second_x_step, 2),
+        (project, -2, 0), (fold, 1, 2), (project, 1, 2), (second_x_step, 4), (fold, 2, 0), (second_z_step, 3),
+        (project, 1, 0), (fold, 2, 1), (first_z_step, 1, 3), (swap_bit, 1), (swap_bit, 2), (second_x_end, 2),
+        (first_z_step, 3, 0), (second_x_end, 1), (project, 2, 0), (second_x_end, 0), (first_z_step, 2, 1),
+        (project, -3, 0), (project, 1, 3), (fold, 2, 2), (fold, 3, 0), (first_z_step, 2, 2),
+        (second_z_step, 4), (project, 2, 1), (second_x_end, 4), (project, 0, 2), (project, 1, 1),
+        (second_x_step, 3), (project, 3, 0), (swap_bit, 3), (first_z_step, 2, 3), (first_z_step, 4, 0),
+        (project, 4, 0), (project, 2, 2), (fold, 3, 1), (fold, 3, 2), (second_x_step, 6), (project, 0, 3),
+        (project, -1, 2), (first_z_step, 3, 1), (project, -2, 2), (project, -1, 3), (second_x_step, 5),
+        (first_z_step, 3, 2), (project, 3, 1), (project, -3, 2), (project, 2, 3), (project, -2, 1),
+        (second_x_end, 3), (second_x_step, 7), (first_z_step, 3, 3), (project, -3, 1), (project, -2, 3),
+        (second_x_end, 6), (project, 3, 3), (first_z_step, 4, 1), (first_z_step, 4, 2), (project, -1, 0),
+        (second_x_end, 5), (project, 4, 2), (project, 3, 2), (project, 4, 1), (project, -3, 3),
+        (first_z_step, 4, 3), (second_x_end, 7), (project, 4, 3),
     ]
     for step in order:
         step[0](*step[1:])
@@ -401,7 +402,7 @@
 
 def attention_kernel(
     table_ref, bias_ref, gathered, values, stationary, words,
-    num_ref, den_ref, num_acc, den_acc, even_weights, odd_weights,
+    num_ref, den_ref, num_acc, den_acc, even_scores, odd_scores, even_weights, odd_weights,
 ):
     pairs = table_ref[3, 0]
     num_acc[...] = jnp.zeros_like(num_acc)
@@ -409,10 +410,10 @@
     odd_weights[...] = jnp.zeros_like(odd_weights)
     bit_of = jnp.left_shift(jnp.int32(1), lax.broadcasted_iota(jnp.int32, (8, TILE), 0))
     half_bias = [bias_ref[h] * 0.5 for h in range(HEADS)]
-
-    def weigh(p, weights):
+    ones = jnp.ones((STRIP, 2 * TILE), jnp.bfloat16)
+
+    def score(p, scores):
         a = table_ref[1, 2 * p]
-        slots = [table_ref[0, 2 * p + u] for u in range(2)]
         sources = jnp.concatenate(
             [
                 gathered[pl.ds(pl.multiple_of(table_ref[2, 2 * p + u] * TILE, TILE), TILE), :]
@@ -422,34 +423,37 @@
         )
 
         def part(half):
-            scores = jnp.dot(
-                sources, stationary[a, :, half * 2 * TILE : (half + 1) * 2 * TILE],
-                preferred_element_type=jnp.float32,
+            lanes = slice(half * 2 * TILE, (half + 1) * 2 * TILE)
+            scores[:, lanes] = jnp.dot(
+                sources, stationary[a, :, lanes], preferred_element_type=jnp.float32
             )
-            total = [jnp.zeros((8, TILE), jnp.float32) for _ in range(2)]
-            for u, s in enumerate(slots):
-                live = jnp.where(s >= 0, bit_of, 0)
-                s = jnp.maximum(s, 0)
-                for g in range(TILE // STRIP):
-                    edge = [
-                        (jnp.broadcast_to(words[w, pl.ds(s, 1), :], (8, TILE)) & live) != 0
-                        for w in (2 * g, 2 * g + 1)
-                    ]
-                    here = slice(u * TILE + g * STRIP, u * TILE + (g + 1) * STRIP)
-                    for side in range(2):
-                        h = half * 2 + side
-                        score = scores[here, side * TILE : (side + 1) * TILE]
-                        twice = jnp.tanh(score + half_bias[h]) + 1.0
-                        low = jnp.where(edge[0], twice[0:8], 0.0)
-                        high = jnp.where(edge[1], twice[8:16], 0.0)
-                        total[side] += low + high
-                        weights[here, h * TILE : (h + 1) * TILE] = jnp.concatenate(
-                            [low, high], axis=0
-                        ).astype(jnp.bfloat16)
-            for side in range(2):
-                den_acc[a, half * 2 + side] += total[side]
 
         return [functools.partial(part, half) for half in range(2)]
+
+    def weigh(p, scores, weights):
+        def part(u, groups):
+            s = table_ref[0, 2 * p + u]
+            live = jnp.where(s >= 0, bit_of, 0)
+            s = jnp.maximum(s, 0)
+            for g in groups:
+                edge = [
+                    jnp.where(
+                        (jnp.broadcast_to(words[w, pl.ds(s, 1), :], (8, TILE)) & live) != 0, 1.0, 0.0
+                    )
+                    for w in (2 * g, 2 * g + 1)
+                ]
+                edge = jnp.concatenate(edge, axis=0).astype(jnp.bfloat16)
+                here = slice(u * TILE + g * STRIP, u * TILE + (g + 1) * STRIP)
+                for h in range(HEADS):
+                    lanes = slice(h * TILE, (h + 1) * TILE)
+                    twice = jnp.tanh(scores[here, lanes] + half_bias[h]) + 1.0
+                    weights[here, lanes] = twice.astype(jnp.bfloat16) * edge
+
+        half = TILE // STRIP // 2
+        return [
+            functools.partial(part, u, range(v * half, (v + 1) * half))
+            for u in range(2) for v in range(2)
+        ]
 
     def mix(p, weights):
         a = table_ref[1, 2 * p]
@@ -458,6 +462,7 @@
         def part(half):
             rows = slice(half * TILE, (half + 1) * TILE)
             v = jnp.concatenate([values[b, rows, :] for b in source], axis=1)
+            v = jnp.concatenate([v, ones], axis=0)
             both = jnp.dot(
                 v, weights[:, half * 2 * TILE : (half + 1) * 2 * TILE],
                 preferred_element_type=jnp.float32,
@@ -467,26 +472,42 @@
                 num_acc[a, start : start + HEAD, :] += both[
                     side * HEAD : (side + 1) * HEAD, side * TILE : (side + 1) * TILE
                 ]
+            den_acc[a, half] += both[TILE : TILE + 8]
 
         return [functools.partial(part, half) for half in range(2)]
 
-    def together(weighed, mixed):
+    def together(scored, mixed, weighed):
         for k in range(2):
-            weighed[k]()
+            scored[k]()
             mixed[k]()
+        for part in weighed:
+            part()
+
+    for part in score(0, even_scores):
+        part()
 
     def turn(t, _):
-        p = 2 * t
-        together(weigh(p, even_weights), mix(jnp.maximum(p - 1, 0), odd_weights))
-        together(weigh(p + 1, odd_weights), mix(p, even_weights))
+        for u in range(0, UNROLL, 2):
+            p = UNROLL * t + u
+            together(
+                score(p + 1, odd_scores), mix(jnp.maximum(p - 1, 0), odd_weights),
+                weigh(p, even_scores, even_weights),
+            )
+            together(
+                score(p + 2, even_scores), mix(p, even_weights),
+                weigh(p + 1, odd_scores, odd_weights),
+            )
         return 0
 
-    turns = (pairs + 1) // 2
+    turns = (pairs + UNROLL - 1) // UNROLL
     lax.fori_loop(0, turns, turn, 0)
-    for part in mix(jnp.maximum(2 * turns - 1, 0), odd_weights):
+    for part in mix(jnp.maximum(UNROLL * turns - 1, 0), odd_weights):
         part()
     num_ref[...] = (num_acc[...] * 0.5).astype(num_ref.dtype)
-    den_ref[...] = jnp.sum(den_acc[...], axis=2) * 0.5
+    for a in range(den_acc.shape[0]):
+        for h in range(HEADS):
+            lanes = slice(h % 2 * TILE, (h % 2 + 1) * TILE)
+            den_ref[a, h : h + 1, :] = den_acc[a, h // 2, 0:1, lanes] * 0.5
 
 
 def attention(table, bias, gathered, values, stationary, words):
@@ -503,7 +524,9 @@
         out_specs=(vmem, vmem),
         scratch_shapes=[
             pltpu.VMEM((row_tiles, D, TILE), jnp.float32),
-            pltpu.VMEM((row_tiles, HEADS, 8, TILE), jnp.float32),
+            pltpu.VMEM((row_tiles, 2, 8, 2 * TILE), jnp.float32),
+            pltpu.VMEM((2 * TILE, HEADS * TILE), jnp.float32),
+            pltpu.VMEM((2 * TILE, HEADS * TILE), jnp.float32),
             pltpu.VMEM((2 * TILE, HEADS * TILE), jnp.bfloat16),
             pltpu.VMEM((2 * TILE, HEADS * TILE), jnp.bfloat16),
         ],

time: 112 us -> 104 us (0.929)
  Pallas kernels: 105 us -> 97.1 us
    pallas_call x1, Pallas kernels: 36.8 us -> 8.17 us  [attention(): pl.pallas_call(attention_kernel, out_shape=(jax.ShapeDtypeStruct((row_til...]
    pallas_call x1, Pallas kernels: 13.9 us -> 32.2 us  [finish(): pl.pallas_call(finish_kernel, out_shape=jax.ShapeDtypeStruct(features.sha...]
    pallas_call x1, Pallas kernels: 54.1 us -> 56.7 us  [exchange(): pl.pallas_call(exchange_kernel, out_shape=(jax.ShapeDtypeStruct((SITES *...]
where the time goes in v4:
time: 104 us
  Pallas kernels  97.1 us (93%)
  local copies, waits for them, and re-layouts  6.34 us (6%)
    pallas_call x1, Pallas kernels, exchange(): pl.pallas_call(exchange_kernel, out_shape=(jax.ShapeDtypeStruct((SITES *...  56.7 us
    pallas_call x1, Pallas kernels, finish(): pl.pallas_call(finish_kernel, out_shape=jax.ShapeDtypeStruct(features.sha...  32.2 us
    pallas_call x1, Pallas kernels, attention(): pl.pallas_call(attention_kernel, out_shape=(jax.ShapeDtypeStruct((row_til...  8.17 us
    unnamed x19, local copies, waits for them, and re-layouts  6.34 us

profile of v4, /device:TPU:1, one launch (start us, length us, event | category | flops | bytes accessed | tf_op | source)
XLA Modules:
  0.0 104.1 jit_solution(179618391084737177)
XLA Ops:
  0.7 0.0 copy-start
  0.7 1.6 %copy-done = s32[1,256,2048]{2,1,0:T(8,128)S(1)} copy-done((s32[1,256,2048]{2,1,0:T(8,128)S(1)}, s32[1,256,2048]{2,1,0:T(8,128)}, u32[]{:S(2)}) %copy-start) | copy-done | bytes 2097176
  2.2 0.0 copy-start.1
  2.2 1.0 copy-done.1
  3.2 0.0 copy-start.3
  3.2 1.0 copy-done.3
  4.2 0.0 copy-start.5
  4.2 0.7 copy-done.5
  4.9 0.0 copy-start.6
  4.9 0.7 copy-done.6
  5.6 56.7 %exchange.1 = (bf16[24576,256]{1,0:T(8,128)(2,1)S(1)}, bf16[192,256,128]{2,1,0:T(8,128)(2,1)S(1)}, bf16[12,256,512]{2,1,0:T(8,128)(2,1)S(1)}, s32[16,256,128]{2,1,0:T(8,128)S(1)}, s32[8,384]{1,0:T(8,128)S(1)}) custom-call(f32[384,256]{1,0:T(8,128)S(1)} %copy-done.1, s32[256,2048]{1,0:T(8,128)S(1)} %bitcast.4, s32[1,256]{1,0:T(1,128)S(1)} %copy-done.5, ...), custom_call_target="tpu_custom_call" | custom-call | tf_op jit(solution)/shard_map/exchange/pallas_call | solution.py:372
  62.3 0.0 copy-start.8
  62.3 0.6 copy-done.8
  63.0 0.0 copy-start.2
  63.0 0.0 copy-start.4
  63.0 0.0 copy-start.7
  63.0 8.2 %attention.1 = (bf16[12,256,128]{2,1,0:T(8,128)(2,1)S(1)}, f32[12,4,128]{2,1,0:T(4,128)S(1)}) custom-call(s32[8,384]{1,0:T(8,128)S(1)} %get-tuple-element.12.table_ref, f32[4]{0:T(128)S(1)} %copy-done.8, bf16[24576,256]{1,0:T(8,128)(2,1)S(1)} %get-tuple-element.13.gathered, bf16[192,256,128]{2,1,0:T(8,128)(2,1)S(1)} %get-tuple-element.14.values, ...), custom_call_target="tpu_custom_call" | custom-call | tf_op jit(solution)/shard_map/attention/pallas_call | solution.py:517
  71.2 0.0 copy-done.2
  71.2 0.0 copy-done.4
  71.2 0.0 copy-done.7
  71.2 32.2 %finish.1 = f32[384,256]{1,0:T(8,128)S(1)} custom-call(f32[384,256]{1,0:T(8,128)S(1)} %copy-done.2, bf16[4,3,256,128]{3,2,1,0:T(8,128)(2,1)S(1)} %bitcast.5, f32[4,3,4,128]{3,2,1,0:T(4,128)S(1)} %bitcast.6, bf16[256,256]{1,0:T(8,128)(2,1)S(1)} %copy-done.4, f32[1,256]{1,0:T(1,128)S(1)} %bitcast.7), custom_call_target="tpu_custom_call" | custom-call | tf_op jit(solution)/shard_map/finish/pallas_call | solution.py:599
  103.4 0.7 copy.12
Async XLA Ops:
  0.7 1.6 %copy-start = (s32[1,256,2048]{2,1,0:T(8,128)S(1)}, s32[1,256,2048]{2,1,0:T(8,128)}, u32[]{:S(2)}) copy-start(s32[1,256,2048]{2,1,0:T(8,128)} %param.16) | copy-start | bytes 6291460
  2.2 1.0 copy-start.1
  3.2 1.0 copy-start.3
  4.2 0.7 copy-start.5
  4.9 0.7 copy-start.6
  62.3 0.7 copy-start.8
  63.0 8.2 %copy-start.2 = (f32[384,256]{1,0:T(8,128)S(1)}, f32[384,256]{1,0:T(8,128)}, u32[]{:S(2)}) copy-start(f32[384,256]{1,0:T(8,128)} %features_ref.3) | copy-start | bytes 1179652
  63.0 8.2 %copy-start.4 = (bf16[256,256]{1,0:T(8,128)(2,1)S(1)}, bf16[256,256]{1,0:T(8,128)(2,1)}, u32[]{:S(2)}) copy-start(bf16[256,256]{1,0:T(8,128)(2,1)} %w_ref.1) | copy-start | bytes 393220
  63.0 8.2 %copy-start.7 = (f32[256]{0:T(256)S(1)}, f32[256]{0:T(256)}, u32[]{:S(2)}) copy-start(f32[256]{0:T(256)} %param.13) | copy-start | bytes 3076

commit v5 on v4

--- a/solution.py
+++ b/solution.py
@@ -12,7 +12,7 @@
 HEAD = 64
 D = 256
 STRIP = 16
-UNROLL = 4
+UNROLL = 12
 TABLE = 384
 NX, NY, NZ = 4, 4, 8
 SITES = NX * NZ
@@ -56,7 +56,7 @@
 
 
 def exchange_kernel(
-    features_ref, masks_ref, rows_ref, cols_ref, count_ref, weights_ref,
+    features_ref, masks_ref, lists_ref, count_ref, weights_ref,
     gathered, values, stationary, words, table,
     queries, own, own_queries, wq, wv, bits, landed, sorted_slots, diagonal,
     query_send, query_recv, list_send, list_recv,
@@ -176,9 +176,9 @@
             spread(c)
 
     def sort_slots():
-        slots = rows_ref.shape[1]
+        slots = lists_ref.shape[1]
         row_tiles = NY * BLOCK
-        to, source = rows_ref[...].astype(jnp.float32), cols_ref[...].astype(jnp.float32)
+        to, source = (lists_ref[k : k + 1, :].astype(jnp.float32) for k in range(2))
         count = jnp.full((1, slots), count_ref[0], jnp.int32).astype(jnp.float32)
         slot = lax.broadcasted_iota(jnp.int32, (1, slots), 1).astype(jnp.float32)
         a = to - row_tiles * jnp.floor((to + 0.5) * (1.0 / row_tiles))
@@ -319,23 +319,23 @@
         pltpu.make_async_copy(gathered.at[pl.ds(0, count)], gathered.at[pl.ds(0, count)], sem).wait()
 
     order = [
-        (second_z_step, 1), (fold, 0, 0), (fold, 0, 1), (fold, 0, 2), (first_z_step, 1, 0), (first_x_step, 2),
-        (second_x_step, 0), (first_x_step, 0, 1), (second_z_step, 2), (start_words,), (fold, 1, 0),
-        (swap_bit, 0), (project, 0, 0), (project, 0, 1), (first_z_step, 2, 0), (first_z_step, 1, 1),
-        (first_z_step, 1, 2), (second_x_step, 1), (project, -1, 1), (fold, 1, 1), (second_x_step, 2),
-        (project, -2, 0), (fold, 1, 2), (project, 1, 2), (second_x_step, 4), (fold, 2, 0), (second_z_step, 3),
-        (project, 1, 0), (fold, 2, 1), (first_z_step, 1, 3), (swap_bit, 1), (swap_bit, 2), (second_x_end, 2),
-        (first_z_step, 3, 0), (second_x_end, 1), (project, 2, 0), (second_x_end, 0), (first_z_step, 2, 1),
-        (project, -3, 0), (project, 1, 3), (fold, 2, 2), (fold, 3, 0), (first_z_step, 2, 2),
-        (second_z_step, 4), (project, 2, 1), (second_x_end, 4), (project, 0, 2), (project, 1, 1),
-        (second_x_step, 3), (project, 3, 0), (swap_bit, 3), (first_z_step, 2, 3), (first_z_step, 4, 0),
-        (project, 4, 0), (project, 2, 2), (fold, 3, 1), (fold, 3, 2), (second_x_step, 6), (project, 0, 3),
-        (project, -1, 2), (first_z_step, 3, 1), (project, -2, 2), (project, -1, 3), (second_x_step, 5),
-        (first_z_step, 3, 2), (project, 3, 1), (project, -3, 2), (project, 2, 3), (project, -2, 1),
-        (second_x_end, 3), (second_x_step, 7), (first_z_step, 3, 3), (project, -3, 1), (project, -2, 3),
-        (second_x_end, 6), (project, 3, 3), (first_z_step, 4, 1), (first_z_step, 4, 2), (project, -1, 0),
-        (second_x_end, 5), (project, 4, 2), (project, 3, 2), (project, 4, 1), (project, -3, 3),
-        (first_z_step, 4, 3), (second_x_end, 7), (project, 4, 3),
+        (project, 0, 0), (second_z_step, 1), (first_x_step, 0, 1), (second_z_step, 2), (second_x_step, 0),
+        (fold, 0, 0), (fold, 0, 1), (first_z_step, 1, 0), (first_z_step, 1, 1), (project, 1, 0), (fold, 0, 2),
+        (first_x_step, 2), (second_x_step, 1), (second_x_step, 2), (fold, 1, 0), (project, 0, 1),
+        (fold, 1, 1), (fold, 1, 2), (fold, 2, 0), (second_z_step, 3), (fold, 2, 1), (fold, 2, 2),
+        (project, 0, 2), (first_z_step, 1, 2), (project, -1, 1), (fold, 3, 0), (first_z_step, 1, 3),
+        (second_x_step, 3), (first_z_step, 2, 0), (project, -2, 0), (second_x_end, 0), (start_words,),
+        (swap_bit, 0), (swap_bit, 1), (first_z_step, 2, 2), (second_x_end, 1), (second_z_step, 4),
+        (project, 1, 1), (swap_bit, 2), (first_z_step, 2, 1), (project, 2, 0), (fold, 3, 1),
+        (second_x_step, 4), (project, 0, 3), (project, 1, 2), (first_z_step, 2, 3), (swap_bit, 3),
+        (project, -1, 3), (second_x_step, 6), (project, -1, 0), (project, -1, 2), (project, 2, 1),
+        (project, -2, 2), (first_z_step, 3, 0), (second_x_step, 5), (second_x_end, 3), (project, 3, 0),
+        (project, -2, 1), (first_z_step, 3, 2), (project, -3, 0), (first_z_step, 3, 1), (project, -2, 3),
+        (project, 2, 2), (second_x_step, 7), (project, 3, 2), (second_x_end, 2), (second_x_end, 4),
+        (first_z_step, 3, 3), (project, -3, 2), (project, 2, 3), (second_x_end, 6), (project, 3, 1),
+        (fold, 3, 2), (first_z_step, 4, 0), (project, -3, 1), (project, 1, 3), (second_x_end, 5),
+        (project, -3, 3), (project, 4, 0), (project, 3, 3), (first_z_step, 4, 2), (first_z_step, 4, 1),
+        (project, 4, 1), (project, 4, 2), (second_x_end, 7), (first_z_step, 4, 3), (project, 4, 3),
     ]
     for step in order:
         step[0](*step[1:])
@@ -363,7 +363,7 @@
         to_partner(sorted_slots, table, 2).wait_send()
 
 
-def exchange(features, masks, tile_rows, tile_cols, tile_count, weights):
+def exchange(features, masks, lists, tile_count, weights):
     slots, length = masks.shape
     vmem = pl.BlockSpec(memory_space=pltpu.VMEM)
     smem = pl.BlockSpec(memory_space=pltpu.SMEM)
@@ -378,7 +378,7 @@
             jax.ShapeDtypeStruct((length // TILE, slots, TILE), jnp.int32),
             jax.ShapeDtypeStruct((8, TABLE), jnp.int32),
         ),
-        in_specs=[vmem, vmem, vmem, vmem, smem, vmem],
+        in_specs=[vmem, vmem, vmem, smem, vmem],
         out_specs=(vmem,) * 5,
         scratch_shapes=[
             pltpu.VMEM((NY, BLOCK, D, TILE), half),
@@ -397,7 +397,7 @@
             collective_id=0, has_side_effects=True, vmem_limit_bytes=16 * 1024 * 1024
         ),
         name="exchange",
-    )(features, masks, tile_rows, tile_cols, tile_count, weights)
+    )(features, masks, lists, tile_count, weights)
 
 
 def attention_kernel(
@@ -544,36 +544,50 @@
     meet(site_partners(z, x, y, core))
     home = y_lo == core
 
-    def part(d, src, dst, k):
+    tiles = NODES // TILE
+
+    def part(d, t):
         c = (y + d) % NY
+        if t < tiles:
+            src, dst = num_ref.at[c, t], nums.at[y, t]
+        else:
+            src, dst = den_ref.at[c], dens.at[y]
         return pltpu.make_async_remote_copy(
-            src_ref=src.at[c], dst_ref=dst.at[y], send_sem=send.at[k, d], recv_sem=recv.at[k, y],
+            src_ref=src, dst_ref=dst, send_sem=send.at[d, t], recv_sem=recv.at[y, t],
             device_id=device(z, x, c // 2 * 2 + core, c % 2), device_id_type=MESH,
         )
 
-    pairs = ((num_ref, nums), (den_ref, dens))
-    for d in (1, 2, 3):
-        for k, (src, dst) in enumerate(pairs):
-            part(d, src, dst, k).start()
-    for k, (src, dst) in enumerate(pairs):
+    order = (tiles,) + tuple(range(tiles))
+    for t in order:
+        for d in (2, 1, 3):
+            part(d, t).start()
+
         @pl.when(home)
         def _():
-            pltpu.make_async_copy(src.at[y], dst.at[y], recv.at[k, y]).start()
+            if t < tiles:
+                src, dst = num_ref.at[y, t], nums.at[y, t]
+            else:
+                src, dst = den_ref.at[y], dens.at[y]
+            pltpu.make_async_copy(src, dst, recv.at[y, t]).start()
 
         @pl.when(jnp.logical_not(home))
         def _():
-            part(0, src, dst, k).start()
-
-    for c in range(NY):
-        for k, (src, dst) in enumerate(pairs):
-            pltpu.make_async_copy(dst.at[c], dst.at[c], recv.at[k, c]).wait()
-    total = sum(nums[c].astype(jnp.float32) for c in range(NY))
+            part(0, t).start()
+
+    def come(t):
+        for c in range(NY):
+            here = nums.at[c, t] if t < tiles else dens.at[c]
+            pltpu.make_async_copy(here, here, recv.at[c, t]).wait()
+
+    come(tiles)
     weight = 1.0 + sum(dens[c] for c in range(NY))
     gain = gain_ref[...]
     node, lane_node = lane_order()
     to_nodes = jnp.transpose(jnp.where(node == lane_node, 1.0, 0.0)).astype(jnp.bfloat16)
     for t in range(NODES // TILE):
-        mixed = total[t].reshape(HEADS, HEAD, TILE) / weight[t].reshape(HEADS, 1, TILE)
+        come(t)
+        total = sum(nums[c, t].astype(jnp.float32) for c in range(NY))
+        mixed = total.reshape(HEADS, HEAD, TILE) / weight[t].reshape(HEADS, 1, TILE)
         mixed = mixed.reshape(D, TILE).astype(jnp.bfloat16)
         mixed = jnp.dot(mixed, to_nodes, preferred_element_type=jnp.float32).astype(jnp.bfloat16)
         projected = lax.dot_general(
@@ -582,14 +596,13 @@
         square = jnp.mean(projected * projected, axis=1, keepdims=True)
         here = pl.ds(t * TILE, TILE)
         out_ref[here, :] = features_ref[here, :] + gain * projected * lax.rsqrt(square + 1e-05)
-    for d in range(NY):
-        for k, (src, dst) in enumerate(pairs):
-            if d:
-                part(d, src, dst, k).wait_send()
-            else:
-                @pl.when(jnp.logical_not(home))
-                def _():
-                    part(d, src, dst, k).wait_send()
+    for t in order:
+        for d in (1, 2, 3):
+            part(d, t).wait_send()
+
+        @pl.when(jnp.logical_not(home))
+        def _():
+            part(0, t).wait_send()
 
 
 def finish(features, numerator, denominator, w_out, gain):
@@ -604,7 +617,7 @@
         scratch_shapes=[
             pltpu.VMEM(numerator.shape, numerator.dtype),
             pltpu.VMEM(denominator.shape, denominator.dtype),
-            dma((2, NY)), dma((2, NY)),
+            dma((NY, 4)), dma((NY, 4)),
         ],
         compiler_params=pltpu.CompilerParams(
             collective_id=1, has_side_effects=True, vmem_limit_bytes=32 * 1024 * 1024
@@ -618,7 +631,7 @@
 ):
     block_tiles = features.shape[0] // TILE
     gathered, values, stationary, words, table = exchange(
-        features, tile_masks[0], tile_rows, tile_cols, tile_count, w_qkv
+        features, tile_masks[0], jnp.concatenate([tile_rows, tile_cols], axis=0), tile_count, w_qkv
     )
     numerator, denominator = attention(
         table, head_bias, gathered, values, stationary, words

time: 104 us -> 99.1 us (0.953)
  Pallas kernels: 97.1 us -> 92.4 us
  local copies, waits for them, and re-layouts: 6.34 us -> 4.99 us
    pallas_call x1, Pallas kernels: 32.2 us -> 23.6 us  [finish(): pl.pallas_call(finish_kernel, out_shape=jax.ShapeDtypeStruct(features.sha...]
    pallas_call x1, Pallas kernels: 8.17 us -> 13.2 us  [attention(): pl.pallas_call(attention_kernel, out_shape=(jax.ShapeDtypeStruct((row_til...]
    unnamed x19 -> x15, local copies, waits for them, and re-layouts: 6.34 us -> 4.99 us
where the time goes in v5:
time: 99.1 us; the launch traced here: 98.8 us
  Pallas kernels  92.4 us (93%)
  local copies, waits for them, and re-layouts  4.99 us (5%)
    pallas_call x1, Pallas kernels, exchange(): pl.pallas_call(exchange_kernel, out_shape=(jax.ShapeDtypeStruct((SITES *...  55.7 us
    pallas_call x1, Pallas kernels, finish(): pl.pallas_call(finish_kernel, out_shape=jax.ShapeDtypeStruct(features.sha...  23.6 us
    pallas_call x1, Pallas kernels, attention(): pl.pallas_call(attention_kernel, out_shape=(jax.ShapeDtypeStruct((row_til...  13.2 us
    unnamed x15, local copies, waits for them, and re-layouts  4.99 us

profile of v5, /device:TPU:1, one launch (start us, length us, event | category | flops | bytes accessed | tf_op | source)
XLA Modules:
  0.0 98.8 jit_solution(3889680661791969414)
XLA Ops:
  0.7 0.7 pad_add_fusion.lists_ref
  1.4 0.0 copy-start
  1.4 1.6 %copy-done = s32[1,256,2048]{2,1,0:T(8,128)S(1)} copy-done((s32[1,256,2048]{2,1,0:T(8,128)S(1)}, s32[1,256,2048]{2,1,0:T(8,128)}, u32[]{:S(2)}) %copy-start) | copy-done | bytes 2097176
  2.9 0.0 copy-start.1
  3.0 1.0 %copy-done.1 = f32[384,256]{1,0:T(8,128)S(1)} copy-done((f32[384,256]{1,0:T(8,128)S(1)}, f32[384,256]{1,0:T(8,128)}, u32[]{:S(2)}) %copy-start.1) | copy-done | bytes 393240
  3.9 0.0 copy-start.3
  3.9 1.0 %copy-done.3 = bf16[256,768]{1,0:T(8,128)(2,1)S(1)} copy-done((bf16[256,768]{1,0:T(8,128)(2,1)S(1)}, bf16[256,768]{1,0:T(8,128)(2,1)}, u32[]{:S(2)}) %copy-start.3) | copy-done | bytes 393240
  4.9 55.7 %exchange.1 = (bf16[24576,256]{1,0:T(8,128)(2,1)S(1)}, bf16[192,256,128]{2,1,0:T(8,128)(2,1)S(1)}, bf16[12,256,512]{2,1,0:T(8,128)(2,1)S(1)}, s32[16,256,128]{2,1,0:T(8,128)S(1)}, s32[8,384]{1,0:T(8,128)S(1)}) custom-call(f32[384,256]{1,0:T(8,128)S(1)} %copy-done.1, s32[256,2048]{1,0:T(8,128)S(1)} %bitcast.4, s32[2,256]{1,0:T(2,128)S(1)} %pad_add_fusion.lists_ref, ...), custom_call_target="tpu_custom_call" | custom-call | tf_op jit(solution)/shard_map/exchange/pallas_call | solution.py:372
  60.6 0.0 copy-start.6
  60.7 0.6 copy-done.6
  61.3 0.0 copy-start.2
  61.3 0.0 copy-start.4
  61.3 0.0 copy-start.5
  61.3 13.2 %attention.1 = (bf16[12,256,128]{2,1,0:T(8,128)(2,1)S(1)}, f32[12,4,128]{2,1,0:T(4,128)S(1)}) custom-call(s32[8,384]{1,0:T(8,128)S(1)} %get-tuple-element.12.table_ref, f32[4]{0:T(128)S(1)} %copy-done.6, bf16[24576,256]{1,0:T(8,128)(2,1)S(1)} %get-tuple-element.13.gathered, bf16[192,256,128]{2,1,0:T(8,128)(2,1)S(1)} %get-tuple-element.14.values, ...), custom_call_target="tpu_custom_call" | custom-call | tf_op jit(solution)/shard_map/attention/pallas_call | solution.py:517
  74.5 0.0 copy-done.2
  74.5 0.0 copy-done.4
  74.5 0.0 copy-done.5
  74.5 23.6 %finish.1 = f32[384,256]{1,0:T(8,128)S(1)} custom-call(f32[384,256]{1,0:T(8,128)S(1)} %copy-done.2, bf16[4,3,256,128]{3,2,1,0:T(8,128)(2,1)S(1)} %bitcast.5, f32[4,3,4,128]{3,2,1,0:T(4,128)S(1)} %bitcast.6, bf16[256,256]{1,0:T(8,128)(2,1)S(1)} %copy-done.4, f32[1,256]{1,0:T(1,128)S(1)} %bitcast.7), custom_call_target="tpu_custom_call" | custom-call | tf_op jit(solution)/shard_map/finish/pallas_call | solution.py:612
  98.1 0.7 copy.12
Async XLA Ops:
  1.4 1.6 %copy-start = (s32[1,256,2048]{2,1,0:T(8,128)S(1)}, s32[1,256,2048]{2,1,0:T(8,128)}, u32[]{:S(2)}) copy-start(s32[1,256,2048]{2,1,0:T(8,128)} %param.16) | copy-start | bytes 6291460
  2.9 1.0 %copy-start.1 = (f32[384,256]{1,0:T(8,128)S(1)}, f32[384,256]{1,0:T(8,128)}, u32[]{:S(2)}) copy-start(f32[384,256]{1,0:T(8,128)} %features_ref.3) | copy-start | bytes 1179652
  3.9 1.0 %copy-start.3 = (bf16[256,768]{1,0:T(8,128)(2,1)S(1)}, bf16[256,768]{1,0:T(8,128)(2,1)}, u32[]{:S(2)}) copy-start(bf16[256,768]{1,0:T(8,128)(2,1)} %weights_ref.1) | copy-start | bytes 1179652
  60.6 0.7 copy-start.6
  61.3 13.2 %copy-start.2 = (f32[384,256]{1,0:T(8,128)S(1)}, f32[384,256]{1,0:T(8,128)}, u32[]{:S(2)}) copy-start(f32[384,256]{1,0:T(8,128)} %features_ref.3) | copy-start | bytes 1179652
  61.3 13.2 %copy-start.4 = (bf16[256,256]{1,0:T(8,128)(2,1)S(1)}, bf16[256,256]{1,0:T(8,128)(2,1)}, u32[]{:S(2)}) copy-start(bf16[256,256]{1,0:T(8,128)(2,1)} %w_ref.1) | copy-start | bytes 393220
  61.3 13.2 %copy-start.5 = (f32[256]{0:T(256)S(1)}, f32[256]{0:T(256)}, u32[]{:S(2)}) copy-start(f32[256]{0:T(256)} %param.13) | copy-start | bytes 3076

commit v6 on v4

--- a/solution.py
+++ b/solution.py
@@ -12,7 +12,7 @@
 HEAD = 64
 D = 256
 STRIP = 16
-UNROLL = 4
+UNROLL = 12
 TABLE = 384
 NX, NY, NZ = 4, 4, 8
 SITES = NX * NZ
@@ -56,7 +56,7 @@
 
 
 def exchange_kernel(
-    features_ref, masks_ref, rows_ref, cols_ref, count_ref, weights_ref,
+    features_ref, masks_ref, lists_ref, count_ref, weights_ref,
     gathered, values, stationary, words, table,
     queries, own, own_queries, wq, wv, bits, landed, sorted_slots, diagonal,
     query_send, query_recv, list_send, list_recv,
@@ -176,9 +176,9 @@
             spread(c)
 
     def sort_slots():
-        slots = rows_ref.shape[1]
+        slots = lists_ref.shape[1]
         row_tiles = NY * BLOCK
-        to, source = rows_ref[...].astype(jnp.float32), cols_ref[...].astype(jnp.float32)
+        to, source = (lists_ref[k : k + 1, :].astype(jnp.float32) for k in range(2))
         count = jnp.full((1, slots), count_ref[0], jnp.int32).astype(jnp.float32)
         slot = lax.broadcasted_iota(jnp.int32, (1, slots), 1).astype(jnp.float32)
         a = to - row_tiles * jnp.floor((to + 0.5) * (1.0 / row_tiles))
@@ -302,40 +302,43 @@
         for e in range(2):
             arrived(a, FIRST + e * HALF2, HALF2, second_x.at[k, e, 1])
 
-    def project(dz, k):
-        a = site_of(dz, X_OFF[k])
-        start = pl.multiple_of((a * 2 + core) * NODES, NODES)
-        tile = (a * 2 + core) * BLOCK
-        forward(a, 0, NODES, sibling_send.at[0], sibling_recv.at[0], other)
-        v = lax.dot_general(
-            wv[...], gathered[pl.ds(start, NODES), :], NT, preferred_element_type=jnp.float32
-        ).astype(jnp.bfloat16)
-        for t in range(BLOCK):
-            values[tile + t] = v[:, t * TILE : (t + 1) * TILE]
-        done = values.at[pl.ds(tile, BLOCK)]
-        remote(done, done, sibling_send.at[1], sibling_recv.at[1], other)
+    def project(*blocks):
+        sites = [site_of(dz, X_OFF[k]) for dz, k in blocks]
+        for a in sites:
+            forward(a, 0, NODES, sibling_send.at[0], sibling_recv.at[0], other)
+        found = [
+            lax.dot_general(
+                wv[...], gathered[rows(a, core, 0, NODES), :], NT, preferred_element_type=jnp.float32
+            ).astype(jnp.bfloat16)
+            for a in sites
+        ]
+        for a, v in zip(sites, found):
+            for t in range(BLOCK):
+                values[(a * 2 + core) * BLOCK + t] = v[:, t * TILE : (t + 1) * TILE]
+        for a in sites:
+            done = values.at[pl.ds((a * 2 + core) * BLOCK, BLOCK)]
+            remote(done, done, sibling_send.at[1], sibling_recv.at[1], other)
 
     def drain(count, sem):
         pltpu.make_async_copy(gathered.at[pl.ds(0, count)], gathered.at[pl.ds(0, count)], sem).wait()
 
     order = [
-        (second_z_step, 1), (fold, 0, 0), (fold, 0, 1), (fold, 0, 2), (first_z_step, 1, 0), (first_x_step, 2),
-        (second_x_step, 0), (first_x_step, 0, 1), (second_z_step, 2), (start_words,), (fold, 1, 0),
-        (swap_bit, 0), (project, 0, 0), (project, 0, 1), (first_z_step, 2, 0), (first_z_step, 1, 1),
-        (first_z_step, 1, 2), (second_x_step, 1), (project, -1, 1), (fold, 1, 1), (second_x_step, 2),
-        (project, -2, 0), (fold, 1, 2), (project, 1, 2), (second_x_step, 4), (fold, 2, 0), (second_z_step, 3),
-        (project, 1, 0), (fold, 2, 1), (first_z_step, 1, 3), (swap_bit, 1), (swap_bit, 2), (second_x_end, 2),
-        (first_z_step, 3, 0), (second_x_end, 1), (project, 2, 0), (second_x_end, 0), (first_z_step, 2, 1),
-        (project, -3, 0), (project, 1, 3), (fold, 2, 2), (fold, 3, 0), (first_z_step, 2, 2),
-        (second_z_step, 4), (project, 2, 1), (second_x_end, 4), (project, 0, 2), (project, 1, 1),
-        (second_x_step, 3), (project, 3, 0), (swap_bit, 3), (first_z_step, 2, 3), (first_z_step, 4, 0),
-        (project, 4, 0), (project, 2, 2), (fold, 3, 1), (fold, 3, 2), (second_x_step, 6), (project, 0, 3),
-        (project, -1, 2), (first_z_step, 3, 1), (project, -2, 2), (project, -1, 3), (second_x_step, 5),
-        (first_z_step, 3, 2), (project, 3, 1), (project, -3, 2), (project, 2, 3), (project, -2, 1),
-        (second_x_end, 3), (second_x_step, 7), (first_z_step, 3, 3), (project, -3, 1), (project, -2, 3),
-        (second_x_end, 6), (project, 3, 3), (first_z_step, 4, 1), (first_z_step, 4, 2), (project, -1, 0),
-        (second_x_end, 5), (project, 4, 2), (project, 3, 2), (project, 4, 1), (project, -3, 3),
-        (first_z_step, 4, 3), (second_x_end, 7), (project, 4, 3),
+        (second_z_step, 1), (first_x_step, 0, 1), (first_z_step, 1, 0), (second_z_step, 2), (fold, 0, 0),
+        (second_x_step, 0), (fold, 0, 1), (first_x_step, 2), (fold, 0, 2), (project, (1, 0), (-1, 0)),
+        (project, (0, 0), (0, 1)), (fold, 1, 0), (second_x_step, 2), (fold, 1, 1), (second_x_step, 1),
+        (first_z_step, 1, 1), (fold, 1, 2), (first_z_step, 2, 0), (project, (2, 0), (-2, 0)), (fold, 2, 0),
+        (first_z_step, 1, 2), (fold, 2, 1), (project, (1, 1), (-1, 1)), (second_z_step, 3), (start_words,),
+        (first_z_step, 1, 3), (swap_bit, 0), (project, (1, 2), (-1, 2)), (swap_bit, 1), (fold, 2, 2),
+        (fold, 3, 0), (second_x_step, 3), (second_x_end, 0), (second_x_end, 1), (second_x_step, 4),
+        (swap_bit, 2), (first_z_step, 2, 1), (project, (0, 2), (0, 3)), (project, (2, 1), (-2, 1)),
+        (first_z_step, 2, 2), (second_z_step, 4), (fold, 3, 1), (swap_bit, 3), (second_x_end, 2),
+        (first_z_step, 2, 3), (fold, 3, 2), (project, (1, 3), (-1, 3)), (second_x_end, 3), (second_x_step, 6),
+        (second_x_step, 5), (first_z_step, 3, 1), (project, (3, 1), (-3, 1)), (first_z_step, 3, 0),
+        (second_x_end, 4), (project, (3, 0), (-3, 0)), (first_z_step, 3, 2), (project, (3, 2), (-3, 2)),
+        (second_x_step, 7), (first_z_step, 3, 3), (project, (2, 3), (-2, 3)), (project, (2, 2), (-2, 2)),
+        (second_x_end, 6), (second_x_end, 5), (project, (3, 3), (-3, 3)), (first_z_step, 4, 0),
+        (first_z_step, 4, 1), (first_z_step, 4, 2), (project, (4, 0), (4, 1)), (first_z_step, 4, 3),
+        (second_x_end, 7), (project, (4, 2), (4, 3)),
     ]
     for step in order:
         step[0](*step[1:])
@@ -363,7 +366,7 @@
         to_partner(sorted_slots, table, 2).wait_send()
 
 
-def exchange(features, masks, tile_rows, tile_cols, tile_count, weights):
+def exchange(features, masks, lists, tile_count, weights):
     slots, length = masks.shape
     vmem = pl.BlockSpec(memory_space=pltpu.VMEM)
     smem = pl.BlockSpec(memory_space=pltpu.SMEM)
@@ -378,7 +381,7 @@
             jax.ShapeDtypeStruct((length // TILE, slots, TILE), jnp.int32),
             jax.ShapeDtypeStruct((8, TABLE), jnp.int32),
         ),
-        in_specs=[vmem, vmem, vmem, vmem, smem, vmem],
+        in_specs=[vmem, vmem, vmem, smem, vmem],
         out_specs=(vmem,) * 5,
         scratch_shapes=[
             pltpu.VMEM((NY, BLOCK, D, TILE), half),
@@ -397,7 +400,7 @@
             collective_id=0, has_side_effects=True, vmem_limit_bytes=16 * 1024 * 1024
         ),
         name="exchange",
-    )(features, masks, tile_rows, tile_cols, tile_count, weights)
+    )(features, masks, lists, tile_count, weights)
 
 
 def attention_kernel(
@@ -618,7 +621,7 @@
 ):
     block_tiles = features.shape[0] // TILE
     gathered, values, stationary, words, table = exchange(
-        features, tile_masks[0], tile_rows, tile_cols, tile_count, w_qkv
+        features, tile_masks[0], jnp.concatenate([tile_rows, tile_cols], axis=0), tile_count, w_qkv
     )
     numerator, denominator = attention(
         table, head_bias, gathered, values, stationary, words

time: 104 us -> 96.7 us (0.930)
  Pallas kernels: 97.1 us -> 90 us
  local copies, waits for them, and re-layouts: 6.34 us -> 4.99 us
    pallas_call x1, Pallas kernels: 32.2 us -> 28.7 us  [finish(): pl.pallas_call(finish_kernel, out_shape=jax.ShapeDtypeStruct(features.sha...]
    pallas_call x1, Pallas kernels: 56.7 us -> 54.2 us  [exchange(): pl.pallas_call(exchange_kernel, out_shape=(jax.ShapeDtypeStruct((SITES *...]
    unnamed x19 -> x15, local copies, waits for them, and re-layouts: 6.34 us -> 4.99 us
where the time goes in v6:
time: 96.7 us; the launch traced here: 96.4 us
  Pallas kernels  90 us (93%)
  local copies, waits for them, and re-layouts  4.99 us (5%)
    pallas_call x1, Pallas kernels, exchange(): pl.pallas_call(exchange_kernel, out_shape=(jax.ShapeDtypeStruct((SITES *...  54.2 us
    pallas_call x1, Pallas kernels, finish(): pl.pallas_call(finish_kernel, out_shape=jax.ShapeDtypeStruct(features.sha...  28.7 us
    pallas_call x1, Pallas kernels, attention(): pl.pallas_call(attention_kernel, out_shape=(jax.ShapeDtypeStruct((row_til...  7.19 us
    unnamed x15, local copies, waits for them, and re-layouts  4.99 us

profile of v6, /device:TPU:1, one launch (start us, length us, event | category | flops | bytes accessed | tf_op | source)
XLA Modules:
  0.0 96.4 jit_solution(7225099826420454398)
XLA Ops:
  0.7 0.7 pad_add_fusion.lists_ref
  1.4 0.0 copy-start
  1.4 1.6 %copy-done = s32[1,256,2048]{2,1,0:T(8,128)S(1)} copy-done((s32[1,256,2048]{2,1,0:T(8,128)S(1)}, s32[1,256,2048]{2,1,0:T(8,128)}, u32[]{:S(2)}) %copy-start) | copy-done | bytes 2097176
  2.9 0.0 copy-start.1
  3.0 1.0 %copy-done.1 = f32[384,256]{1,0:T(8,128)S(1)} copy-done((f32[384,256]{1,0:T(8,128)S(1)}, f32[384,256]{1,0:T(8,128)}, u32[]{:S(2)}) %copy-start.1) | copy-done | bytes 393240
  3.9 0.0 copy-start.3
  3.9 1.0 %copy-done.3 = bf16[256,768]{1,0:T(8,128)(2,1)S(1)} copy-done((bf16[256,768]{1,0:T(8,128)(2,1)S(1)}, bf16[256,768]{1,0:T(8,128)(2,1)}, u32[]{:S(2)}) %copy-start.3) | copy-done | bytes 393240
  4.9 54.2 %exchange.1 = (bf16[24576,256]{1,0:T(8,128)(2,1)S(1)}, bf16[192,256,128]{2,1,0:T(8,128)(2,1)S(1)}, bf16[12,256,512]{2,1,0:T(8,128)(2,1)S(1)}, s32[16,256,128]{2,1,0:T(8,128)S(1)}, s32[8,384]{1,0:T(8,128)S(1)}) custom-call(f32[384,256]{1,0:T(8,128)S(1)} %copy-done.1, s32[256,2048]{1,0:T(8,128)S(1)} %bitcast.4, s32[2,256]{1,0:T(2,128)S(1)} %pad_add_fusion.lists_ref, ...), custom_call_target="tpu_custom_call" | custom-call | tf_op jit(solution)/shard_map/exchange/pallas_call | solution.py:375
  59.1 0.0 copy-start.6
  59.1 0.6 copy-done.6
  59.8 0.0 copy-start.2
  59.8 0.0 copy-start.4
  59.8 0.0 copy-start.5
  59.8 7.2 %attention.1 = (bf16[12,256,128]{2,1,0:T(8,128)(2,1)S(1)}, f32[12,4,128]{2,1,0:T(4,128)S(1)}) custom-call(s32[8,384]{1,0:T(8,128)S(1)} %get-tuple-element.12.table_ref, f32[4]{0:T(128)S(1)} %copy-done.6, bf16[24576,256]{1,0:T(8,128)(2,1)S(1)} %get-tuple-element.13.gathered, bf16[192,256,128]{2,1,0:T(8,128)(2,1)S(1)} %get-tuple-element.14.values, ...), custom_call_target="tpu_custom_call" | custom-call | tf_op jit(solution)/shard_map/attention/pallas_call | solution.py:520
  67.0 0.0 copy-done.2
  67.0 0.0 copy-done.4
  67.0 0.0 copy-done.5
  67.0 28.7 %finish.1 = f32[384,256]{1,0:T(8,128)S(1)} custom-call(f32[384,256]{1,0:T(8,128)S(1)} %copy-done.2, bf16[4,3,256,128]{3,2,1,0:T(8,128)(2,1)S(1)} %bitcast.5, f32[4,3,4,128]{3,2,1,0:T(4,128)S(1)} %bitcast.6, bf16[256,256]{1,0:T(8,128)(2,1)S(1)} %copy-done.4, f32[1,256]{1,0:T(1,128)S(1)} %bitcast.7), custom_call_target="tpu_custom_call" | custom-call | tf_op jit(solution)/shard_map/finish/pallas_call | solution.py:602
  95.7 0.7 copy.12
Async XLA Ops:
  1.4 1.6 %copy-start = (s32[1,256,2048]{2,1,0:T(8,128)S(1)}, s32[1,256,2048]{2,1,0:T(8,128)}, u32[]{:S(2)}) copy-start(s32[1,256,2048]{2,1,0:T(8,128)} %param.16) | copy-start | bytes 6291460
  2.9 1.0 %copy-start.1 = (f32[384,256]{1,0:T(8,128)S(1)}, f32[384,256]{1,0:T(8,128)}, u32[]{:S(2)}) copy-start(f32[384,256]{1,0:T(8,128)} %features_ref.3) | copy-start | bytes 1179652
  3.9 1.0 %copy-start.3 = (bf16[256,768]{1,0:T(8,128)(2,1)S(1)}, bf16[256,768]{1,0:T(8,128)(2,1)}, u32[]{:S(2)}) copy-start(bf16[256,768]{1,0:T(8,128)(2,1)} %weights_ref.1) | copy-start | bytes 1179652
  59.1 0.7 copy-start.6
  59.8 7.2 %copy-start.2 = (f32[384,256]{1,0:T(8,128)S(1)}, f32[384,256]{1,0:T(8,128)}, u32[]{:S(2)}) copy-start(f32[384,256]{1,0:T(8,128)} %features_ref.3) | copy-start | bytes 1179652
  59.8 7.2 %copy-start.4 = (bf16[256,256]{1,0:T(8,128)(2,1)S(1)}, bf16[256,256]{1,0:T(8,128)(2,1)}, u32[]{:S(2)}) copy-start(bf16[256,256]{1,0:T(8,128)(2,1)} %w_ref.1) | copy-start | bytes 393220
  59.8 7.2 %copy-start.5 = (f32[256]{0:T(256)S(1)}, f32[256]{0:T(256)}, u32[]{:S(2)}) copy-start(f32[256]{0:T(256)} %param.13) | copy-start | bytes 3076

commit v7 on v6

--- a/solution.py
+++ b/solution.py
@@ -12,7 +12,7 @@
 HEAD = 64
 D = 256
 STRIP = 16
-UNROLL = 12
+UNROLL = 22
 TABLE = 384
 NX, NY, NZ = 4, 4, 8
 SITES = NX * NZ
@@ -144,7 +144,6 @@
             own_queries[t] = jnp.dot(
                 q[:, t * TILE : (t + 1) * TILE], to_lanes, preferred_element_type=jnp.float32
             ).astype(jnp.bfloat16)
-        sort_slots()
 
     def fold(c, t):
         if t == 0:
@@ -174,6 +173,8 @@
         handed(landed, 1)
         for c in range(words.shape[0]):
             spread(c)
+
+    placed = []
 
     def sort_slots():
         slots = lists_ref.shape[1]
@@ -202,6 +203,10 @@
             jnp.where((across_lanes == down) & earlier, 1.0, 0.0), axis=0, keepdims=True
         )
         at = jnp.where(a < row_tiles, base + rank, float(TABLE))
+        placed.extend([slots, row_tiles, slot, a, b, total, at])
+
+    def list_slots():
+        slots, row_tiles, slot, a, b, total, at = placed
         at_down = jnp.transpose(jnp.broadcast_to(at, (TABLE, slots)))
         hit = at_down == lax.broadcasted_iota(jnp.int32, (slots, TABLE), 1).astype(jnp.float32)
 
@@ -214,6 +219,7 @@
         sorted_slots[2:3, :] = pick(b).astype(jnp.int32)
         sorted_slots[3:4, :] = jnp.broadcast_to(total * 0.5, (1, TABLE)).astype(jnp.int32)
         sorted_slots[4:8, :] = jnp.zeros((4, TABLE), jnp.int32)
+        hand_over(sorted_slots, table, 2)
 
     hand_over(own, gathered.at[rows(site, y_lo, 0, NODES)], 0)
 
@@ -242,7 +248,6 @@
     for d in (1, 2, 3):
         to_queries(d).start()
     hand_over(bits, landed, 1)
-    hand_over(sorted_slots, table, 2)
 
     X_OFF = (0, -1, 1, 2)
     Z_OFF = (0, -1, 1, -2, 2, -3, 3, 4)
@@ -323,22 +328,23 @@
         pltpu.make_async_copy(gathered.at[pl.ds(0, count)], gathered.at[pl.ds(0, count)], sem).wait()
 
     order = [
-        (second_z_step, 1), (first_x_step, 0, 1), (first_z_step, 1, 0), (second_z_step, 2), (fold, 0, 0),
-        (second_x_step, 0), (fold, 0, 1), (first_x_step, 2), (fold, 0, 2), (project, (1, 0), (-1, 0)),
-        (project, (0, 0), (0, 1)), (fold, 1, 0), (second_x_step, 2), (fold, 1, 1), (second_x_step, 1),
-        (first_z_step, 1, 1), (fold, 1, 2), (first_z_step, 2, 0), (project, (2, 0), (-2, 0)), (fold, 2, 0),
-        (first_z_step, 1, 2), (fold, 2, 1), (project, (1, 1), (-1, 1)), (second_z_step, 3), (start_words,),
-        (first_z_step, 1, 3), (swap_bit, 0), (project, (1, 2), (-1, 2)), (swap_bit, 1), (fold, 2, 2),
-        (fold, 3, 0), (second_x_step, 3), (second_x_end, 0), (second_x_end, 1), (second_x_step, 4),
-        (swap_bit, 2), (first_z_step, 2, 1), (project, (0, 2), (0, 3)), (project, (2, 1), (-2, 1)),
-        (first_z_step, 2, 2), (second_z_step, 4), (fold, 3, 1), (swap_bit, 3), (second_x_end, 2),
-        (first_z_step, 2, 3), (fold, 3, 2), (project, (1, 3), (-1, 3)), (second_x_end, 3), (second_x_step, 6),
-        (second_x_step, 5), (first_z_step, 3, 1), (project, (3, 1), (-3, 1)), (first_z_step, 3, 0),
-        (second_x_end, 4), (project, (3, 0), (-3, 0)), (first_z_step, 3, 2), (project, (3, 2), (-3, 2)),
-        (second_x_step, 7), (first_z_step, 3, 3), (project, (2, 3), (-2, 3)), (project, (2, 2), (-2, 2)),
-        (second_x_end, 6), (second_x_end, 5), (project, (3, 3), (-3, 3)), (first_z_step, 4, 0),
-        (first_z_step, 4, 1), (first_z_step, 4, 2), (project, (4, 0), (4, 1)), (first_z_step, 4, 3),
-        (second_x_end, 7), (project, (4, 2), (4, 3)),
+        (second_z_step, 1), (first_x_step, 0, 1), (first_z_step, 1, 0), (fold, 0, 0), (second_z_step, 2),
+        (fold, 0, 1), (second_x_step, 0), (first_x_step, 2), (fold, 0, 2), (project, (1, 0), (-1, 0)),
+        (fold, 1, 0), (project, (0, 0), (0, 1)), (fold, 1, 1), (fold, 1, 2), (second_x_step, 1),
+        (sort_slots,), (first_z_step, 1, 1), (second_x_step, 2), (first_z_step, 2, 0),
+        (project, (2, 0), (-2, 0)), (list_slots,), (first_z_step, 1, 2), (fold, 2, 0), (fold, 2, 1),
+        (project, (1, 1), (-1, 1)), (second_z_step, 3), (start_words,), (first_z_step, 1, 3),
+        (project, (1, 2), (-1, 2)), (swap_bit, 0), (fold, 2, 2), (second_x_step, 3), (swap_bit, 1),
+        (fold, 3, 0), (second_x_end, 0), (second_x_end, 1), (second_x_step, 4), (first_z_step, 2, 1),
+        (swap_bit, 2), (project, (2, 1), (-2, 1)), (first_z_step, 2, 2), (project, (0, 2), (0, 3)),
+        (second_z_step, 4), (fold, 3, 1), (second_x_end, 2), (project, (1, 3), (-1, 3)), (first_z_step, 2, 3),
+        (fold, 3, 2), (swap_bit, 3), (second_x_end, 3), (first_z_step, 3, 0), (second_x_step, 5),
+        (second_x_step, 6), (first_z_step, 3, 1), (project, (3, 1), (-3, 1)), (second_x_end, 4),
+        (project, (3, 0), (-3, 0)), (first_z_step, 3, 2), (project, (3, 2), (-3, 2)), (second_x_step, 7),
+        (first_z_step, 3, 3), (project, (2, 2), (-2, 2)), (project, (2, 3), (-2, 3)), (second_x_end, 5),
+        (second_x_end, 6), (project, (3, 3), (-3, 3)), (first_z_step, 4, 0), (first_z_step, 4, 1),
+        (first_z_step, 4, 2), (project, (4, 0), (4, 1)), (second_x_end, 7), (first_z_step, 4, 3),
+        (project, (4, 2), (4, 3)),
     ]
     for step in order:
         step[0](*step[1:])

time: 96.7 us -> 96.1 us (level)
    pallas_call x1, Pallas kernels: 28.7 us -> 14.2 us  [finish(): pl.pallas_call(finish_kernel, out_shape=jax.ShapeDtypeStruct(features.sha...]
    pallas_call x1, Pallas kernels: 7.19 us -> 21.5 us  [attention(): pl.pallas_call(attention_kernel, out_shape=(jax.ShapeDtypeStruct((row_til...]
where the time goes in v7:
time: 96.1 us; the launch traced here: 96 us
  Pallas kernels  89.6 us (93%)
  local copies, waits for them, and re-layouts  4.99 us (5%)
    pallas_call x1, Pallas kernels, exchange(): pl.pallas_call(exchange_kernel, out_shape=(jax.ShapeDtypeStruct((SITES *...  54 us
    pallas_call x1, Pallas kernels, attention(): pl.pallas_call(attention_kernel, out_shape=(jax.ShapeDtypeStruct((row_til...  21.5 us
    pallas_call x1, Pallas kernels, finish(): pl.pallas_call(finish_kernel, out_shape=jax.ShapeDtypeStruct(features.sha...  14.2 us
    unnamed x15, local copies, waits for them, and re-layouts  4.99 us

profile of v7, /device:TPU:1, one launch (start us, length us, event | category | flops | bytes accessed | tf_op | source)
XLA Modules:
  0.0 96.0 jit_solution(8615889776501683922)
XLA Ops:
  0.7 0.7 pad_add_fusion.lists_ref
  1.4 0.0 copy-start
  1.4 1.6 %copy-done = s32[1,256,2048]{2,1,0:T(8,128)S(1)} copy-done((s32[1,256,2048]{2,1,0:T(8,128)S(1)}, s32[1,256,2048]{2,1,0:T(8,128)}, u32[]{:S(2)}) %copy-start) | copy-done | bytes 2097176
  2.9 0.0 copy-start.1
  3.0 1.0 %copy-done.1 = f32[384,256]{1,0:T(8,128)S(1)} copy-done((f32[384,256]{1,0:T(8,128)S(1)}, f32[384,256]{1,0:T(8,128)}, u32[]{:S(2)}) %copy-start.1) | copy-done | bytes 393240
  3.9 0.0 copy-start.3
  3.9 1.0 %copy-done.3 = bf16[256,768]{1,0:T(8,128)(2,1)S(1)} copy-done((bf16[256,768]{1,0:T(8,128)(2,1)S(1)}, bf16[256,768]{1,0:T(8,128)(2,1)}, u32[]{:S(2)}) %copy-start.3) | copy-done | bytes 393240
  4.9 54.0 %exchange.1 = (bf16[24576,256]{1,0:T(8,128)(2,1)S(1)}, bf16[192,256,128]{2,1,0:T(8,128)(2,1)S(1)}, bf16[12,256,512]{2,1,0:T(8,128)(2,1)S(1)}, s32[16,256,128]{2,1,0:T(8,128)S(1)}, s32[8,384]{1,0:T(8,128)S(1)}) custom-call(f32[384,256]{1,0:T(8,128)S(1)} %copy-done.1, s32[256,2048]{1,0:T(8,128)S(1)} %bitcast.4, s32[2,256]{1,0:T(2,128)S(1)} %pad_add_fusion.lists_ref, ...), custom_call_target="tpu_custom_call" | custom-call | tf_op jit(solution)/shard_map/exchange/pallas_call | solution.py:381
  58.9 0.0 copy-start.6
  58.9 0.6 copy-done.6
  59.6 0.0 copy-start.2
  59.6 0.0 copy-start.4
  59.6 0.0 copy-start.5
  59.6 21.5 %attention.1 = (bf16[12,256,128]{2,1,0:T(8,128)(2,1)S(1)}, f32[12,4,128]{2,1,0:T(4,128)S(1)}) custom-call(s32[8,384]{1,0:T(8,128)S(1)} %get-tuple-element.12.table_ref, f32[4]{0:T(128)S(1)} %copy-done.6, bf16[24576,256]{1,0:T(8,128)(2,1)S(1)} %get-tuple-element.13.gathered, bf16[192,256,128]{2,1,0:T(8,128)(2,1)S(1)} %get-tuple-element.14.values, ...), custom_call_target="tpu_custom_call" | custom-call | tf_op jit(solution)/shard_map/attention/pallas_call | solution.py:526
  81.0 0.0 copy-done.2
  81.1 0.0 copy-done.4
  81.1 0.0 copy-done.5
  81.1 14.2 %finish.1 = f32[384,256]{1,0:T(8,128)S(1)} custom-call(f32[384,256]{1,0:T(8,128)S(1)} %copy-done.2, bf16[4,3,256,128]{3,2,1,0:T(8,128)(2,1)S(1)} %bitcast.5, f32[4,3,4,128]{3,2,1,0:T(4,128)S(1)} %bitcast.6, bf16[256,256]{1,0:T(8,128)(2,1)S(1)} %copy-done.4, f32[1,256]{1,0:T(1,128)S(1)} %bitcast.7), custom_call_target="tpu_custom_call" | custom-call | tf_op jit(solution)/shard_map/finish/pallas_call | solution.py:608
  95.3 0.7 copy.12
Async XLA Ops:
  1.4 1.6 %copy-start = (s32[1,256,2048]{2,1,0:T(8,128)S(1)}, s32[1,256,2048]{2,1,0:T(8,128)}, u32[]{:S(2)}) copy-start(s32[1,256,2048]{2,1,0:T(8,128)} %param.16) | copy-start | bytes 6291460
  2.9 1.0 %copy-start.1 = (f32[384,256]{1,0:T(8,128)S(1)}, f32[384,256]{1,0:T(8,128)}, u32[]{:S(2)}) copy-start(f32[384,256]{1,0:T(8,128)} %features_ref.3) | copy-start | bytes 1179652
  3.9 1.0 %copy-start.3 = (bf16[256,768]{1,0:T(8,128)(2,1)S(1)}, bf16[256,768]{1,0:T(8,128)(2,1)}, u32[]{:S(2)}) copy-start(bf16[256,768]{1,0:T(8,128)(2,1)} %weights_ref.1) | copy-start | bytes 1179652
  58.9 0.7 copy-start.6
  59.6 21.5 %copy-start.2 = (f32[384,256]{1,0:T(8,128)S(1)}, f32[384,256]{1,0:T(8,128)}, u32[]{:S(2)}) copy-start(f32[384,256]{1,0:T(8,128)} %features_ref.3) | copy-start | bytes 1179652
  59.6 21.5 %copy-start.4 = (bf16[256,256]{1,0:T(8,128)(2,1)S(1)}, bf16[256,256]{1,0:T(8,128)(2,1)}, u32[]{:S(2)}) copy-start(bf16[256,256]{1,0:T(8,128)(2,1)} %w_ref.1) | copy-start | bytes 393220
  59.6 21.5 %copy-start.5 = (f32[256]{0:T(256)S(1)}, f32[256]{0:T(256)}, u32[]{:S(2)}) copy-start(f32[256]{0:T(256)} %param.13) | copy-start | bytes 3076

commit v8 on v7

--- a/solution.py
+++ b/solution.py
@@ -68,10 +68,6 @@
 
     def setup():
         own[...] = features_ref[...].astype(jnp.bfloat16)
-        wq[...] = jnp.transpose(weights_ref[:, 0:D])
-        wv[...] = jnp.transpose(weights_ref[:, 2 * D : 3 * D])
-        bits[...] = masks_ref[...].astype(jnp.float32).astype(jnp.bfloat16)
-        diagonal[...] = jnp.zeros_like(diagonal)
 
     meet(
         site_partners(z, x, y, core)
@@ -136,6 +132,9 @@
         )
 
     def prepare():
+        wq[...] = jnp.transpose(weights_ref[:, 0:D])
+        wv[...] = jnp.transpose(weights_ref[:, 2 * D : 3 * D])
+        diagonal[...] = jnp.zeros_like(diagonal)
         node, lane_node = lane_order()
         to_lanes = jnp.where(node == lane_node, 1.0, 0.0).astype(jnp.bfloat16)
         q = lax.dot_general(wq[...], own[...], NT, preferred_element_type=jnp.float32)
@@ -247,6 +246,7 @@
 
     for d in (1, 2, 3):
         to_queries(d).start()
+    bits[...] = masks_ref[...].astype(jnp.float32).astype(jnp.bfloat16)
     hand_over(bits, landed, 1)
 
     X_OFF = (0, -1, 1, 2)
@@ -573,14 +573,14 @@
         def _():
             part(0, src, dst, k).start()
 
+    node, lane_node = lane_order()
+    to_nodes = jnp.transpose(jnp.where(node == lane_node, 1.0, 0.0)).astype(jnp.bfloat16)
     for c in range(NY):
         for k, (src, dst) in enumerate(pairs):
             pltpu.make_async_copy(dst.at[c], dst.at[c], recv.at[k, c]).wait()
     total = sum(nums[c].astype(jnp.float32) for c in range(NY))
     weight = 1.0 + sum(dens[c] for c in range(NY))
     gain = gain_ref[...]
-    node, lane_node = lane_order()
-    to_nodes = jnp.transpose(jnp.where(node == lane_node, 1.0, 0.0)).astype(jnp.bfloat16)
     for t in range(NODES // TILE):
         mixed = total[t].reshape(HEADS, HEAD, TILE) / weight[t].reshape(HEADS, 1, TILE)
         mixed = mixed.reshape(D, TILE).astype(jnp.bfloat16)

time: 96.1 us -> 95.4 us (level)
  the two profiles are of different devices: /device:TPU:1 before, /device:TPU:7 now
where the time goes in v8:
time: 95.4 us; the launch traced here: 94.8 us
  Pallas kernels  88.4 us (93%)
  local copies, waits for them, and re-layouts  4.99 us (5%)
    pallas_call x1, Pallas kernels, exchange(): pl.pallas_call(exchange_kernel, out_shape=(jax.ShapeDtypeStruct((SITES *...  53.1 us
    pallas_call x1, Pallas kernels, attention(): pl.pallas_call(attention_kernel, out_shape=(jax.ShapeDtypeStruct((row_til...  21.5 us
    pallas_call x1, Pallas kernels, finish(): pl.pallas_call(finish_kernel, out_shape=jax.ShapeDtypeStruct(features.sha...  13.8 us
    unnamed x15, local copies, waits for them, and re-layouts  4.99 us

profile of v8, /device:TPU:7, one launch (start us, length us, event | category | flops | bytes accessed | tf_op | source)
XLA Modules:
  0.0 94.8 jit_solution(17601689575301361743)
XLA Ops:
  0.7 0.7 pad_add_fusion.lists_ref
  1.4 0.0 copy-start
  1.4 1.6 %copy-done = s32[1,256,2048]{2,1,0:T(8,128)S(1)} copy-done((s32[1,256,2048]{2,1,0:T(8,128)S(1)}, s32[1,256,2048]{2,1,0:T(8,128)}, u32[]{:S(2)}) %copy-start) | copy-done | bytes 2097176
  2.9 0.0 copy-start.1
  3.0 1.0 %copy-done.1 = f32[384,256]{1,0:T(8,128)S(1)} copy-done((f32[384,256]{1,0:T(8,128)S(1)}, f32[384,256]{1,0:T(8,128)}, u32[]{:S(2)}) %copy-start.1) | copy-done | bytes 393240
  3.9 0.0 copy-start.3
  3.9 1.0 %copy-done.3 = bf16[256,768]{1,0:T(8,128)(2,1)S(1)} copy-done((bf16[256,768]{1,0:T(8,128)(2,1)S(1)}, bf16[256,768]{1,0:T(8,128)(2,1)}, u32[]{:S(2)}) %copy-start.3) | copy-done | bytes 393240
  4.9 53.1 %exchange.1 = (bf16[24576,256]{1,0:T(8,128)(2,1)S(1)}, bf16[192,256,128]{2,1,0:T(8,128)(2,1)S(1)}, bf16[12,256,512]{2,1,0:T(8,128)(2,1)S(1)}, s32[16,256,128]{2,1,0:T(8,128)S(1)}, s32[8,384]{1,0:T(8,128)S(1)}) custom-call(f32[384,256]{1,0:T(8,128)S(1)} %copy-done.1, s32[256,2048]{1,0:T(8,128)S(1)} %bitcast.4, s32[2,256]{1,0:T(2,128)S(1)} %pad_add_fusion.lists_ref, ...), custom_call_target="tpu_custom_call" | custom-call | tf_op jit(solution)/shard_map/exchange/pallas_call | solution.py:381
  58.1 0.0 copy-start.6
  58.1 0.6 copy-done.6
  58.7 0.0 copy-start.2
  58.7 0.0 copy-start.4
  58.7 0.0 copy-start.5
  58.7 21.5 %attention.1 = (bf16[12,256,128]{2,1,0:T(8,128)(2,1)S(1)}, f32[12,4,128]{2,1,0:T(4,128)S(1)}) custom-call(s32[8,384]{1,0:T(8,128)S(1)} %get-tuple-element.12.table_ref, f32[4]{0:T(128)S(1)} %copy-done.6, bf16[24576,256]{1,0:T(8,128)(2,1)S(1)} %get-tuple-element.13.gathered, bf16[192,256,128]{2,1,0:T(8,128)(2,1)S(1)} %get-tuple-element.14.values, ...), custom_call_target="tpu_custom_call" | custom-call | tf_op jit(solution)/shard_map/attention/pallas_call | solution.py:526
  80.2 0.0 copy-done.2
  80.2 0.0 copy-done.4
  80.2 0.0 copy-done.5
  80.2 13.8 %finish.1 = f32[384,256]{1,0:T(8,128)S(1)} custom-call(f32[384,256]{1,0:T(8,128)S(1)} %copy-done.2, bf16[4,3,256,128]{3,2,1,0:T(8,128)(2,1)S(1)} %bitcast.5, f32[4,3,4,128]{3,2,1,0:T(4,128)S(1)} %bitcast.6, bf16[256,256]{1,0:T(8,128)(2,1)S(1)} %copy-done.4, f32[1,256]{1,0:T(1,128)S(1)} %bitcast.7), custom_call_target="tpu_custom_call" | custom-call | tf_op jit(solution)/shard_map/finish/pallas_call | solution.py:608
  94.1 0.7 copy.12
Async XLA Ops:
  1.4 1.6 %copy-start = (s32[1,256,2048]{2,1,0:T(8,128)S(1)}, s32[1,256,2048]{2,1,0:T(8,128)}, u32[]{:S(2)}) copy-start(s32[1,256,2048]{2,1,0:T(8,128)} %param.16) | copy-start | bytes 6291460
  2.9 1.0 %copy-start.1 = (f32[384,256]{1,0:T(8,128)S(1)}, f32[384,256]{1,0:T(8,128)}, u32[]{:S(2)}) copy-start(f32[384,256]{1,0:T(8,128)} %features_ref.3) | copy-start | bytes 1179652
  3.9 1.0 %copy-start.3 = (bf16[256,768]{1,0:T(8,128)(2,1)S(1)}, bf16[256,768]{1,0:T(8,128)(2,1)}, u32[]{:S(2)}) copy-start(bf16[256,768]{1,0:T(8,128)(2,1)} %weights_ref.1) | copy-start | bytes 1179652
  58.1 0.7 copy-start.6
  58.7 21.5 %copy-start.2 = (f32[384,256]{1,0:T(8,128)S(1)}, f32[384,256]{1,0:T(8,128)}, u32[]{:S(2)}) copy-start(f32[384,256]{1,0:T(8,128)} %features_ref.3) | copy-start | bytes 1179652
  58.7 21.5 %copy-start.4 = (bf16[256,256]{1,0:T(8,128)(2,1)S(1)}, bf16[256,256]{1,0:T(8,128)(2,1)}, u32[]{:S(2)}) copy-start(bf16[256,256]{1,0:T(8,128)(2,1)} %w_ref.1) | copy-start | bytes 393220
  58.7 21.5 %copy-start.5 = (f32[256]{0:T(256)S(1)}, f32[256]{0:T(256)}, u32[]{:S(2)}) copy-start(f32[256]{0:T(256)} %param.13) | copy-start | bytes 3076
